TPU v7x, 512 devices: a whole 4x8x8 slice. The times are simulated.
512 devices in a mesh: dp: 16 (over z, core), table: 32 (over y, x).
Axes of the slice: x: 4, y: 8, z: 8, core: 2. Of those that a mesh axis runs over, the one named last changes fastest.
Arguments:
- events: bfloat16 [262144, 512], P(('dp', 'table')), may hold values from -6 to 6
- upstream: bfloat16 [262144, 512], P(('dp', 'table')), may hold values from -24 to 24
- w_in: bfloat16 [512, 2048], replicated, may hold values from -0.25 to 0.25
- w_out: bfloat16 [512, 512], replicated, may hold values from -0.25 to 0.25
- lengths: int32 [512, 8], P(('dp', 'table')), may hold values from 1 to 256, 512 in all within a row
- owners: int32 [262144, 1], P(('dp', 'table')), may hold values from 0 to 511; in each aligned block of 512 rows (0 to 511, 512 to 1023, ...) at most 2 rows name the same one
- item_rows: int32 [262144], P(('dp', 'table')), may hold values from 0 to 1023
Outputs:
- out_grad: float32 [512, 512], P('table', 'dp')
- table_grad: bfloat16 [524288, 512], P(('dp', 'table'))
Inputs may be any that keep to these rules, and one draw needn't show every extreme that they name: Each device's lengths sum to 512; each is 1 to 256 and one of them equals 256. `owners`: among the 512 events of one device at most 2 name the same owner, and in some device some owner is named exactly 2 times.
All inputs are finite; a program needn't handle non-finite values.
Results may differ from a plain program's by a relative error of at most 0.0086.
Values may be sent and summed in bfloat16 or wider, within the bound.
A program may use at most 128 MiB of HBM per device.

v0:
```python
import jax
import jax.numpy as jnp
from jax import lax
from jax.sharding import PartitionSpec as P

HEADS = 8
ROWS_DEV = 1024


eps = 1e-06


def normalize(values):
    mean = jnp.mean(values, axis=-1, keepdims=True)
    centered = values - mean
    inverse = lax.rsqrt(jnp.mean(centered * centered, axis=-1, keepdims=True) + eps)
    return (centered * inverse, inverse)


def norm_back(grad, normed, inverse):
    first = jnp.mean(grad, axis=-1, keepdims=True)
    second = jnp.mean(grad * normed, axis=-1, keepdims=True)
    return inverse * (grad - first - normed * second)


def silu_slope(values):
    sig = jax.nn.sigmoid(values)
    return sig * (1.0 + values * (1.0 - sig))


def segment_mask(lengths_row, count):
    ends = jnp.cumsum(lengths_row)
    place = jnp.arange(count, dtype=jnp.int32)
    segment = jnp.sum((place[:, None] >= ends[None, :]).astype(jnp.int32), axis=1)
    same = segment[:, None] == segment[None, :]
    causal = place[None, :] <= place[:, None]
    return jnp.where(same & causal, 1.0 / 64.0, 0.0).astype(jnp.float32)


def layer_grads(events, upstream, w_in, w_out, lengths_row):
    count, width = events.shape
    head_dim = width // HEADS
    scale = 1.0 / float(head_dim) ** 0.5
    f32 = jnp.float32
    x_norm, x_inv = normalize(events.astype(f32))
    normed = x_norm.astype(jnp.bfloat16)
    z_pre = jnp.dot(normed, w_in, preferred_element_type=f32)
    act = jax.nn.silu(z_pre).astype(jnp.bfloat16)
    u_part, v_part, q_part, k_part = jnp.split(act, 4, axis=1)
    mask = segment_mask(lengths_row, count)
    q_heads = q_part.reshape(count, HEADS, head_dim)
    k_heads = k_part.reshape(count, HEADS, head_dim)
    v_heads = v_part.reshape(count, HEADS, head_dim)
    scores = jnp.einsum("qhd,khd->hqk", q_heads, k_heads, preferred_element_type=f32) * scale
    weights = (jax.nn.silu(scores) * mask[None]).astype(jnp.bfloat16)
    attended = jnp.einsum("hqk,khd->qhd", weights, v_heads, preferred_element_type=f32).reshape(
        count, width
    )
    att_norm, att_inv = normalize(attended)
    u_float = u_part.astype(f32)
    gated = (att_norm * u_float).astype(jnp.bfloat16)
    gated_grad = lax.dot_general(
        upstream, w_out, (((1,), (1,)), ((), ())), preferred_element_type=f32
    )
    u_grad = gated_grad * att_norm
    att_grad = norm_back(gated_grad * u_float, att_norm, att_inv).astype(jnp.bfloat16)
    att_heads = att_grad.reshape(count, HEADS, head_dim)
    weight_grad = jnp.einsum("qhd,khd->hqk", att_heads, v_heads, preferred_element_type=f32)
    v_grad = jnp.einsum("hqk,qhd->khd", weights, att_heads, preferred_element_type=f32)
    score_grad = (weight_grad * mask[None] * silu_slope(scores) * scale).astype(jnp.bfloat16)
    q_grad = jnp.einsum("hqk,khd->qhd", score_grad, k_heads, preferred_element_type=f32)
    k_grad = jnp.einsum("hqk,qhd->khd", score_grad, q_heads, preferred_element_type=f32)
    joined = jnp.concatenate(
        [
            u_grad,
            v_grad.reshape(count, width),
            q_grad.reshape(count, width),
            k_grad.reshape(count, width),
        ],
        axis=1,
    )
    z_grad = (joined * silu_slope(z_pre)).astype(jnp.bfloat16)
    normed_grad = lax.dot_general(
        z_grad, w_in, (((1,), (1,)), ((), ())), preferred_element_type=f32
    )
    event_grad = (upstream.astype(f32) + norm_back(normed_grad, x_norm, x_inv)).astype(jnp.bfloat16)
    return (gated, event_grad)


def local(events, upstream, w_in, w_out, lengths, owners, item_rows):
    gated, event_grad = layer_grads(events, upstream, w_in, w_out, lengths[0])
    n_dp = lax.axis_size("dp")
    n_table = lax.axis_size("table")
    count, width = events.shape
    row_share = lax.psum_scatter(
        lax.dot_general(
            gated, upstream, (((0,), (0,)), ((), ())), preferred_element_type=jnp.float32
        ),
        "table",
        scatter_dimension=0,
        tiled=True,
    )
    out_grad = lax.psum_scatter(row_share, "dp", scatter_dimension=1, tiled=True)
    owner = owners[:, 0]
    place = jnp.arange(count, dtype=jnp.int32)
    earlier = (owner[None, :] == owner[:, None]) & (place[None, :] < place[:, None])
    rank = jnp.sum(earlier.astype(jnp.int32), axis=1)
    devices = n_dp * n_table
    slots_cap = max(2, 2 * count // devices)
    empty_rows = jnp.full((devices * slots_cap,), -1, jnp.int32)
    empty_data = jnp.zeros((devices * slots_cap, width), jnp.bfloat16)
    slot = owner * slots_cap + rank
    send_data = empty_data.at[slot].set(event_grad).reshape(n_dp, n_table, slots_cap, width)
    send_rows = empty_rows.at[slot].set(item_rows).reshape(n_dp, n_table, slots_cap)
    moved_data, moved_rows = (
        lax.all_to_all(send_data, "table", split_axis=1, concat_axis=1, tiled=True),
        lax.all_to_all(send_rows, "table", split_axis=1, concat_axis=1, tiled=True),
    )
    moved_data, moved_rows = (
        lax.all_to_all(moved_data, "dp", split_axis=0, concat_axis=0, tiled=True),
        lax.all_to_all(moved_rows, "dp", split_axis=0, concat_axis=0, tiled=True),
    )
    flat_data = moved_data.reshape(-1, width)
    flat_rows = moved_rows.reshape(-1)
    local_rows = jnp.arange(ROWS_DEV, dtype=jnp.int32)
    hits = (local_rows[:, None] == flat_rows[None, :]).astype(jnp.bfloat16)
    table_grad = jnp.dot(hits, flat_data, preferred_element_type=jnp.float32).astype(jnp.bfloat16)
    return (out_grad, table_grad)


def solution(mesh):
    placed = (
        P(("dp", "table"), None),
        P(("dp", "table"), None),
        P(),
        P(),
        P(("dp", "table"), None),
        P(("dp", "table"), None),
        P(("dp", "table")),
    )
    return jax.shard_map(
        local,
        mesh=mesh,
        in_specs=placed,
        out_specs=(P("table", "dp"), P(("dp", "table"), None)),
        check_vma=False,
    )
```

profile of v0, /device:TPU:1, one launch (start us, length us, event | category | flops | bytes accessed | tf_op | source)
XLA Modules:
  0.0 410.6 jit_solution(14051268537327819395)
XLA Ops:
  9.0 2.6 scatter_custom_fusion
  12.7 10.5 %all-to-all-start = ((s32[16,32,2]{0,2,1:T(2,128)}), s32[16,32,2]{0,2,1:T(2,128)S(1)}, u32[]{:S(2)}, u32[]{:S(2)}) async-start(s32[16,32,2]{0,2,1:T(2,128)} %copy.96), calls=%async_computation.1 | async-start | bytes 65536 | tf_op jit(solution)/shard_map/all_to_all | solution.py:117
  24.7 3.8 multiply_convert_fusion.2
  30.8 2.1 copy.93
  35.6 7.5 %multiply_convert_fusion.1 = (bf16[8,512,512]{2,1,0:T(8,128)(2,1)S(1)}, f32[8,512,512]{2,1,0:T(8,128)}) fusion(f32[512,512]{1,0:T(8,128)} %fusion.21, bf16[512,8,64]{0,2,1:T(8,128)(2,1)} %bitcast.50, bf16[512,8,64]{0,2,1:T(8,128)(2,1)} %bitcast.52), kind=kOutput, calls=%fused_computation.3 | convolution fusion | flops 283115520 | bytes 14680064 | tf_op jit(solution)/shard_map/qhd,khd->hqk/dot_general | solution.py:54
  43.1 2.0 copy-done.1
  49.0 2.0 fusion.35
  51.0 2.6 fusion.23
  53.6 2.1 copy.102
  55.7 4.3 %fusion.43 = f32[8,64,512]{2,1,0:T(8,128)} fusion(bf16[512,8,64]{0,2,1:T(8,128)(2,1)} %bitcast.56, bf16[8,512,512]{2,1,0:T(8,128)(2,1)} %copy-done.1), kind=kOutput, calls=%fused_computation.71 | convolution fusion | flops 268435456 | bytes 5767168 | tf_op jit(solution)/shard_map/hqk,qhd->khd/dot_general | solution.py:69
  60.0 6.7 %multiply_convert_fusion = bf16[8,512,512]{2,1,0:T(8,128)(2,1)S(1)} fusion(f32[8,512,512]{2,1,0:T(8,128)} %get-tuple-element.14, f32[512,512]{1,0:T(8,128)S(1)} %copy-done.12, bf16[512,8,64]{0,2,1:T(8,128)(2,1)S(1)} %bitcast.57, bf16[512,8,64]{0,2,1:T(8,128)(2,1)S(1)} %bitcast.55), kind=kOutput, calls=%fused_computation.2 | convolution fusion | flops 293601280 | bytes 14680064 | tf_op jit(solution)/shard_map/qhd,khd->hqk/dot_general | solution.py:68
  66.7 2.3 fusion.44
  69.1 1.8 fusion.45
  70.9 2.0 copy.99
  72.9 2.6 copy.103
  75.5 2.5 copy.104
  78.1 2.5 copy.105
  80.6 5.6 %fusion.40 = (f32[512]{0:T(512)S(1)}, f32[512]{0:T(512)S(1)}, f32[512,512]{0,1:T(8,128)S(1)}) fusion(f32[512]{0:T(512)S(1)} %add_rsqrt_fusion.1, f32[512]{0:T(512)S(1)} %broadcast_multiply_fusion.5, bf16[512,512]{0,1:T(8,128)(2,1)} %copy-done.3, bf16[512,2048]{1,0:T(8,128)(2,1)S(1)} %copy-done, f32[512,512]{1,0:T(8,128)} %copy.105, f32[512,512]{1,0:T(8,128)} %copy.104, ...), kind=kOutput, calls=%fused_computation.68 | convolution fusion | flops 1087896576 | bytes 12066816 | tf_op jit(solution)/shard_map/dot_general | solution.py:83
  87.4 2.0 copy.106
  89.4 4.0 scatter_custom_fusion.1
  93.4 2.3 reshape.161
  95.6 3.3 copy.107
  98.9 9.3 %all-to-all-start.2 = ((bf16[16,32,2,512]{3,2,0,1:T(2,128)(2,1)}), bf16[16,32,2,512]{3,2,0,1:T(2,128)(2,1)}, u32[]{:S(2)}, u32[]{:S(2)}) async-start(bf16[16,32,2,512]{3,2,0,1:T(2,128)(2,1)} %copy.107), calls=%async_computation.3 | async-start | bytes 2097152 | tf_op jit(solution)/shard_map/all_to_all | solution.py:116
  108.3 2.8 fusion.24
  111.9 22.1 %all-to-all-done.2 = bf16[16,32,2,512]{3,2,0,1:T(2,128)(2,1)} async-done(((bf16[16,32,2,512]{3,2,0,1:T(2,128)(2,1)}), bf16[16,32,2,512]{3,2,0,1:T(2,128)(2,1)}, u32[]{:S(2)}, u32[]{:S(2)}) %all-to-all-start.2) | async-done | bytes 1048608 | tf_op jit(solution)/shard_map/all_to_all | solution.py:116
  133.9 13.8 %all-to-all-start.1 = ((s32[16,32,2]{1,2,0:T(2,128)}), s32[16,32,2]{1,2,0:T(2,128)S(1)}, u32[]{:S(2)}, u32[]{:S(2)}) async-start(s32[16,32,2]{1,2,0:T(2,128)} %copy.97), calls=%async_computation.2 | async-start | bytes 32768 | tf_op jit(solution)/shard_map/all_to_all | solution.py:121
  147.8 3.2 copy.108
  151.0 4.1 %all-to-all-done.1 = s32[16,32,2]{1,2,0:T(2,128)S(1)} async-done(((s32[16,32,2]{1,2,0:T(2,128)}), s32[16,32,2]{1,2,0:T(2,128)S(1)}, u32[]{:S(2)}, u32[]{:S(2)}) %all-to-all-start.1) | async-done | bytes 4128 | tf_op jit(solution)/shard_map/all_to_all | solution.py:121
  155.1 3.8 all-to-all-start.3
  159.0 174.8 %reduce-scatter.5.cloned.1.call-done = f32[16,512]{1,0:T(8,128)} async-done(((f32[512,512]{1,0:T(8,128)}), f32[16,512]{1,0:T(8,128)}) %reduce-scatter.5.cloned.1.call-update) | async-done | bytes 32784 | tf_op jit(solution)/shard_map/reduce_scatter | solution.py:95
  335.7 62.0 %reduce-scatter.7.cloned.1.call-done = f32[32,16]{1,0:T(8,128)} async-done(((f32[512,16]{1,0:T(8,128)}), f32[32,16]{1,0:T(8,128)}) %reduce-scatter.7.cloned.1.call-update) | async-done | bytes 2064
  400.3 3.4 fusion.5
  (63 shorter events, 19.8 us)
Async XLA Ops:
  7.2 17.6 %copy-start = (bf16[512,2048]{1,0:T(8,128)(2,1)S(1)}, bf16[512,2048]{1,0:T(8,128)(2,1)}, u32[]{:S(2)}) copy-start(bf16[512,2048]{1,0:T(8,128)(2,1)} %param.9) | copy-start | bytes 6291460
  12.7 86.3 %all-to-all-start = ((s32[16,32,2]{0,2,1:T(2,128)}), s32[16,32,2]{0,2,1:T(2,128)S(1)}, u32[]{:S(2)}, u32[]{:S(2)}) async-start(s32[16,32,2]{0,2,1:T(2,128)} %copy.96), calls=%async_computation.1 | async-start | bytes 65536 | tf_op jit(solution)/shard_map/all_to_all | solution.py:117
  24.4 4.2 %copy-start.3 = (bf16[512,512]{0,1:T(8,128)(2,1)}, bf16[512,512]{0,1:T(8,128)(2,1)S(1)}, u32[]{:S(2)}) copy-start(bf16[512,512]{0,1:T(8,128)(2,1)S(1)} %copy.91) | copy-start | bytes 1572868
  28.6 1.4 copy-start.5
  28.6 5.4 %copy-start.13 = (s32[1,8]{1,0:T(1,128)S(1)}, s32[1,8]{1,0:T(1,128)}, u32[]{:S(2)}) copy-start(s32[1,8]{1,0:T(1,128)} %param.11) | copy-start | bytes 100
  35.6 7.5 %copy-start.9 = (bf16[512,512]{0,1:T(8,128)(2,1)}, bf16[512,512]{0,1:T(8,128)(2,1)S(1)}, u32[]{:S(2)}) copy-start(bf16[512,512]{0,1:T(8,128)(2,1)S(1)} %copy.92) | copy-start | bytes 1572868
  43.1 2.0 copy-start.1
  46.5 1.0 copy-start.2
  55.7 4.3 %copy-start.10 = (bf16[512,512]{0,1:T(8,128)(2,1)S(1)}, bf16[512,512]{0,1:T(8,128)(2,1)}, u32[]{:S(2)}) copy-start(bf16[512,512]{0,1:T(8,128)(2,1)} %copy-done.9) | copy-start | bytes 1572868
  55.7 4.3 %copy-start.11 = (bf16[512,512]{0,1:T(8,128)(2,1)S(1)}, bf16[512,512]{0,1:T(8,128)(2,1)}, u32[]{:S(2)}) copy-start(bf16[512,512]{0,1:T(8,128)(2,1)} %copy.102) | copy-start | bytes 1572868
  55.7 4.3 %copy-start.12 = (f32[512,512]{1,0:T(8,128)S(1)}, f32[512,512]{1,0:T(8,128)}, u32[]{:S(2)}) copy-start(f32[512,512]{1,0:T(8,128)} %fusion.21) | copy-start | bytes 3145732
  60.0 6.7 %copy-start.8 = (bf16[512,512]{0,1:T(8,128)(2,1)S(1)}, bf16[512,512]{0,1:T(8,128)(2,1)}, u32[]{:S(2)}) copy-start(bf16[512,512]{0,1:T(8,128)(2,1)} %copy.94) | copy-start | bytes 1572868
  66.7 2.4 copy-start.7
  80.6 5.6 %copy-start.4 = (bf16[512,512]{0,1:T(8,128)(2,1)S(1)}, bf16[512,512]{0,1:T(8,128)(2,1)}, u32[]{:S(2)}) copy-start(bf16[512,512]{0,1:T(8,128)(2,1)} %copy-done.3) | copy-start | bytes 1572868
  80.6 5.6 %copy-start.6 = (bf16[512,512]{0,1:T(8,128)(2,1)S(1)}, bf16[512,512]{0,1:T(8,128)(2,1)}, u32[]{:S(2)}) copy-start(bf16[512,512]{0,1:T(8,128)(2,1)} %copy.99) | copy-start | bytes 1572868
  98.9 35.0 %all-to-all-start.2 = ((bf16[16,32,2,512]{3,2,0,1:T(2,128)(2,1)}), bf16[16,32,2,512]{3,2,0,1:T(2,128)(2,1)}, u32[]{:S(2)}, u32[]{:S(2)}) async-start(bf16[16,32,2,512]{3,2,0,1:T(2,128)(2,1)} %copy.107), calls=%async_computation.3 | async-start | bytes 2097152 | tf_op jit(solution)/shard_map/all_to_all | solution.py:116
  108.3 225.5 %reduce-scatter.5.cloned.1.call-start = ((), (), s32[]{:S(2)}) async-start(), calls=%async_computation.6 | async-start | bytes 1081344 | tf_op jit(solution)/shard_map/reduce_scatter | solution.py:95
  133.9 21.2 %all-to-all-start.1 = ((s32[16,32,2]{1,2,0:T(2,128)}), s32[16,32,2]{1,2,0:T(2,128)S(1)}, u32[]{:S(2)}, u32[]{:S(2)}) async-start(s32[16,32,2]{1,2,0:T(2,128)} %copy.97), calls=%async_computation.2 | async-start | bytes 32768 | tf_op jit(solution)/shard_map/all_to_all | solution.py:121
  155.1 244.0 %all-to-all-start.3 = ((bf16[16,32,2,512]{3,2,1,0:T(2,128)(2,1)}), bf16[16,32,2,512]{3,2,1,0:T(2,128)(2,1)S(1)}, u32[]{:S(2)}, u32[]{:S(2)}) async-start(bf16[16,32,2,512]{3,2,1,0:T(2,128)(2,1)} %copy.108), calls=%async_computation.4 | async-start | bytes 2097152 | tf_op jit(solution)/shard_map/all_to_all | solution.py:120
  158.9 238.8 %reduce-scatter.7.cloned.1.call-start = ((), (), s32[]{:S(2)}) async-start(), calls=%async_computation.7 | async-start | bytes 278528
Sparse Core Ops, SparseCore 0:
  114.1 219.6 reduce-scatter.4
  337.1 60.5 reduce-scatter.6
where the time goes:
time: 414 us; the launch traced here: 411 us
  waiting for transfers between devices  263 us (64%)
  local copies, waits for them, and re-layouts  46.6 us (11%)
  matrix products  41.7 us (10%)
  starting transfers between devices  37.6 us (9%)
  between operations  14.2 us (3%)
  other arithmetic  7.49 us (2%)
    reduce_scatter x1, waiting for transfers between devices, local(): lax.psum_scatter(lax.dot_general(gated, upstream, (((0,), (0,)), ((), ())...  175 us
    unnamed x3, waiting for transfers between devices  62 us
    all_to_all x1, waiting for transfers between devices, local(): lax.all_to_all(send_data, 'table', split_axis=1, concat_axis=1, tiled=True)  22.1 us
    all_to_all x1, starting transfers between devices, local(): lax.all_to_all(moved_rows, 'dp', split_axis=0, concat_axis=0, tiled=True)  13.8 us
    all_to_all x1, starting transfers between devices, local(): lax.all_to_all(send_rows, 'table', split_axis=1, concat_axis=1, tiled=True)  10.5 us
    unnamed x32, local copies, waits for them, and re-layouts  10.4 us
    all_to_all x1, starting transfers between devices, local(): lax.all_to_all(send_data, 'table', split_axis=1, concat_axis=1, tiled=True)  9.34 us
  transfers between devices with their start and end apart: 6, of which 4 were waited for; matrix products, arithmetic and copies ran while one was open for 20% of the time, Pallas kernels for 0%

commit v1 on v0

v1 whole, which is shorter than its diff:
```python
import functools
import jax
import jax.numpy as jnp
from jax import lax
from jax.experimental import pallas as pl
from jax.experimental.pallas import tpu as pltpu
from jax.sharding import PartitionSpec as P

HEADS = 8
HD = 64
TOK = 512
D = 512
EPS = 1e-6
F32 = jnp.float32
BF16 = jnp.bfloat16
JB = 128
OUT_OF_MASK = -1e30


def dot_nn(a, b):
    return lax.dot_general(a, b, (((1,), (0,)), ((), ())), preferred_element_type=F32)


def dot_nt(a, b):
    return lax.dot_general(a, b, (((1,), (1,)), ((), ())), preferred_element_type=F32)


def window(jb):
    lo = jb * JB
    return lo, min(TOK, -(-(lo + JB + 255) // 128) * 128)


def build_bias(len_ref, bias_ref):
    ends, total = [], 0
    for n in range(8):
        total = total + len_ref[0, n]
        ends.append(total)
    col = lax.broadcasted_iota(jnp.int32, (TOK, 1), 0)
    row = lax.broadcasted_iota(jnp.int32, (1, TOK), 1)
    seg_col = jnp.zeros((TOK, 1), jnp.int32)
    seg_row = jnp.zeros((1, TOK), jnp.int32)
    for n in range(8):
        seg_col = seg_col + (col >= ends[n]).astype(jnp.int32)
        seg_row = seg_row + (row >= ends[n]).astype(jnp.int32)
    for jb in range(TOK // JB):
        lo, hi = window(jb)
        keep = (seg_col[lo:lo + JB] == seg_row[:, lo:hi]) & (col[lo:lo + JB] <= row[:, lo:hi])
        bias_ref[lo:lo + JB, lo:hi] = jnp.where(keep, 0.0, OUT_OF_MASK)


def zero_corners(ref, lead):
    zeros = jnp.zeros(lead + (128, 128), ref.dtype)
    full = (slice(None),) * len(lead)
    ref[full + (slice(0, 128), slice(384, 512))] = zeros
    ref[full + (slice(128, 256), slice(0, 128))] = zeros
    ref[full + (slice(384, 512), slice(256, 384))] = zeros


def normalize_events(ev_ref, xnt_ref, normedt_ref, inv_ref):
    x = ev_ref[...].T.astype(F32)
    mean = jnp.mean(x, axis=0, keepdims=True)
    c = x - mean
    inv = lax.rsqrt(jnp.mean(c * c, axis=0, keepdims=True) + EPS)
    xn = c * inv
    xnt_ref[...] = xn
    normedt_ref[...] = xn.astype(BF16)
    inv_ref[...] = inv


def project(w_in_ref, normedt_ref, slope_ref, act_ref):
    for c in range(16):
        lo = c * 128
        wt = w_in_ref[:, lo:lo + 128].T
        half = dot_nn(wt, normedt_ref[...]) * 0.5
        t = jnp.tanh(half)
        p = 1.0 + t
        act = half * p
        slope_ref[lo:lo + 128, :] = p + act * (1.0 - t)
        act_ref[lo:lo + 128, :] = act.astype(BF16)


def natural(act_ref, nat_ref):
    nat_ref[:, 0:512] = act_ref[512:1024, :].T
    nat_ref[:, 512:1024] = act_ref[1536:2048, :].T


def head_pair_cols(nat_ref, base, pair):
    return nat_ref[:, pl.ds(pl.multiple_of(base + pair * 128, 128), 128)]


def attend_head(h, act_ref, bias_ref, w_ref, dsl_ref, att_ref):
    r = pl.multiple_of(h * HD, HD)
    qt = act_ref[pl.ds(1024 + r, HD), :] * 0.0625
    kt = act_ref[pl.ds(1536 + r, HD), :]
    vt = act_ref[pl.ds(512 + r, HD), :] * (1.0 / 64.0)
    k = kt.T
    for jb in range(TOK // JB):
        lo, hi = window(jb)
        half = dot_nn(k[lo:lo + JB], qt[:, lo:hi]) + bias_ref[lo:lo + JB, lo:hi]
        t = jnp.tanh(half)
        p = 1.0 + t
        w = half * p
        w_ref[h, lo:lo + JB, lo:hi] = w.astype(BF16)
        dsl_ref[h, lo:lo + JB, lo:hi] = p + w * (1.0 - t)
    att_ref[pl.ds(r, HD), 0:256] = dot_nn(vt[:, 0:256], w_ref[h, 0:256, 0:256])
    att_ref[pl.ds(r, HD), 256:512] = dot_nn(vt, w_ref[h, :, 256:512])


def norm_att(att_ref, ainv_ref, act_ref, gated_ref):
    a = att_ref[...]
    mean = jnp.mean(a, axis=0, keepdims=True)
    c = a - mean
    inv = lax.rsqrt(jnp.mean(c * c, axis=0, keepdims=True) + EPS)
    an = c * inv
    att_ref[...] = an
    ainv_ref[...] = inv
    gated_ref[...] = (an * act_ref[0:512, :].astype(F32)).astype(BF16)


def att_backward(w_out_ref, up_ref, att_ref, ainv_ref, act_ref, slope_ref, zg_ref, ag_ref):
    gg = dot_nt(w_out_ref[...], up_ref[...])
    an = att_ref[...]
    zg_ref[0:512, :] = (gg * an * slope_ref[0:512, :]).astype(BF16)
    g = gg * act_ref[0:512, :].astype(F32)
    first = jnp.mean(g, axis=0, keepdims=True)
    second = jnp.mean(g * an, axis=0, keepdims=True)
    ag_ref[...] = ((g - first - an * second) * (ainv_ref[...] * (1.0 / 128.0))).astype(BF16)


def backward_head(h, act_ref, ag_ref, w_ref, dsl_ref, ds_ref, slope_ref, zg_ref):
    r = pl.multiple_of(h * HD, HD)
    qt = act_ref[pl.ds(1024 + r, HD), :]
    kt = act_ref[pl.ds(1536 + r, HD), :]
    v = act_ref[pl.ds(512 + r, HD), :].T
    ag = ag_ref[pl.ds(r, HD), :]
    for jb in range(TOK // JB):
        lo, hi = window(jb)
        wg = dot_nn(v[lo:lo + JB], ag[:, lo:hi])
        ds_ref[lo:lo + JB, lo:hi] = (wg * dsl_ref[h, lo:lo + JB, lo:hi]).astype(BF16)
    vg0 = dot_nt(ag, w_ref[h, 0:256, :])
    vg1 = dot_nt(ag[:, 256:512], w_ref[h, 256:512, 256:512])
    zg_ref[pl.ds(512 + r, HD), 0:256] = (vg0 * 2.0 * slope_ref[pl.ds(512 + r, HD), 0:256]).astype(BF16)
    zg_ref[pl.ds(512 + r, HD), 256:512] = (vg1 * 2.0 * slope_ref[pl.ds(512 + r, HD), 256:512]).astype(BF16)
    qg0 = dot_nn(kt[:, 0:256], ds_ref[0:256, 0:256])
    qg1 = dot_nn(kt, ds_ref[:, 256:512])
    zg_ref[pl.ds(1024 + r, HD), 0:256] = (qg0 * 0.125 * slope_ref[pl.ds(1024 + r, HD), 0:256]).astype(BF16)
    zg_ref[pl.ds(1024 + r, HD), 256:512] = (qg1 * 0.125 * slope_ref[pl.ds(1024 + r, HD), 256:512]).astype(BF16)
    kg0 = dot_nt(qt, ds_ref[0:256, :])
    kg1 = dot_nt(qt[:, 256:512], ds_ref[256:512, 256:512])
    zg_ref[pl.ds(1536 + r, HD), 0:256] = (kg0 * 0.125 * slope_ref[pl.ds(1536 + r, HD), 0:256]).astype(BF16)
    zg_ref[pl.ds(1536 + r, HD), 256:512] = (kg1 * 0.125 * slope_ref[pl.ds(1536 + r, HD), 256:512]).astype(BF16)


def event_gradient(w_in_ref, zg_ref, up_ref, xnt_ref, inv_ref, eg_ref):
    ng = dot_nn(w_in_ref[...], zg_ref[...])
    xn = xnt_ref[...]
    first = jnp.mean(ng, axis=0, keepdims=True)
    second = jnp.mean(ng * xn, axis=0, keepdims=True)
    back = (ng - first - xn * second) * (inv_ref[...] * 0.5)
    eg_ref[...] = (up_ref[...].T.astype(F32) + back).astype(BF16)


MESH = pl.DeviceIdType.MESH
SLOTS = 1024
ROWS_DEV = 1024
CHUNKS = 4
CW = D // CHUNKS


def log2(n):
    return n.bit_length() - 1


def one_hot(rows, cols_of):
    at = lax.broadcasted_iota(jnp.int32, (rows, cols_of.shape[1]), 0)
    return jnp.where(at == cols_of, 1.0, 0.0).astype(BF16)


def start_all(axis, size, rows, src_ref, dst_ref, send_sem, recv_sem):
    me = lax.axis_index(axis)
    mine = pl.ds(pl.multiple_of(me * rows, rows), rows)
    pltpu.make_async_copy(src_ref.at[mine], dst_ref.at[mine], recv_sem).start()

    def send(k, carry):
        peer = lax.rem(me + k, size)
        pltpu.make_async_remote_copy(
            src_ref=src_ref.at[pl.ds(pl.multiple_of(peer * rows, rows), rows)],
            dst_ref=dst_ref.at[mine],
            send_sem=send_sem,
            recv_sem=recv_sem,
            device_id={axis: peer},
            device_id_type=MESH,
        ).start()
        return carry

    lax.fori_loop(1, size, send, 0)


def wait_bytes(ref, sem):
    pltpu.make_async_copy(ref, ref, sem).wait()


def route_slots(owner_ref, item_ref, n_dp, n_table, oh_a, oh_b, meta_ref):
    cap = SLOTS // (n_dp * n_table)
    row = owner_ref[...]
    col = jnp.broadcast_to(row, (128, TOK)).T[:, 0:1]
    place_col = lax.broadcasted_iota(jnp.int32, (TOK, 1), 0)
    place_row = lax.broadcasted_iota(jnp.int32, (1, TOK), 1)
    earlier = (col == row) & (place_col < place_row)
    rank = jnp.sum(jnp.where(earlier, 1.0, 0.0), axis=0, keepdims=True).astype(jnp.int32)
    table, dp = row & (n_table - 1), row >> log2(n_table)
    oh_a[...] = one_hot(SLOTS, table * (n_dp * cap) + dp * cap + rank)
    oh_b[...] = one_hot(SLOTS, dp * (n_table * cap) + table * cap + rank)
    code = item_ref[...] + 1
    line = lax.broadcasted_iota(jnp.int32, (128, TOK), 0)
    high, low = (code >> 5).astype(F32), (code & 31).astype(F32)
    meta_t = jnp.where(line == 0, high, jnp.where(line == 1, low, 0.0)).astype(BF16)
    meta_ref[...] = dot_nt(oh_a[...], meta_t).astype(BF16)


def build_swap(first, second, cap, ref):
    out = lax.broadcasted_iota(jnp.int32, (SLOTS, 1), 0)
    slot = out & (cap - 1)
    a = (out >> log2(cap)) & (first - 1)
    b = out >> (log2(cap) + log2(first))
    at = lax.broadcasted_iota(jnp.int32, (SLOTS, SLOTS), 1)
    ref[...] = jnp.where(at == a * (second * cap) + b * cap + slot, 1.0, 0.0).astype(BF16)


def build_hits(meta, ref):
    lines = meta.astype(F32).T
    item = (lines[0:1] * 32.0 + lines[1:2] - 1.0).astype(jnp.int32)
    ref[...] = one_hot(ROWS_DEV, item)


def kernel(n_dp, n_table, *refs):
    names = INPUTS + OUTPUTS + tuple(scratch(n_dp, n_table))
    r = dict(zip(names, refs))
    ns = type("Refs", (), r)
    dp, table = lax.axis_index("dp"), lax.axis_index("table")
    core = lax.rem(dp, 2)
    cap = SLOTS // (n_dp * n_table)
    row_share, col_share, half_dp = D // n_table, D // n_dp, n_dp // 2

    barrier = pltpu.get_barrier_semaphore()
    for axis, size, me in (("table", n_table, table), ("dp", n_dp, dp)):
        def greet(k, carry, axis=axis, size=size, me=me):
            pl.semaphore_signal(
                barrier, inc=1, device_id={axis: lax.rem(me + k, size)}, device_id_type=MESH
            )
            return carry
        lax.fori_loop(1, size, greet, 0)

    route_slots(ns.owners, ns.items, n_dp, n_table, ns.oh_a, ns.oh_b, ns.meta.at[0])
    pl.semaphore_wait(barrier, n_table + n_dp - 2)
    start_all("table", n_table, n_dp * cap, ns.meta.at[0], ns.meta.at[1], ns.send.at[0], ns.recv.at[0])

    build_bias(ns.lengths, ns.bias)
    zero_corners(ns.w, (HEADS,))
    zero_corners(ns.ds, ())
    build_swap(n_table, n_dp, cap, ns.swap_a)
    build_swap(n_dp, n_table, cap, ns.swap_b)
    normalize_events(ns.events, ns.xnt, ns.normedt, ns.inv)
    project(ns.w_in, ns.normedt, ns.slope, ns.act)

    wait_bytes(ns.meta.at[1], ns.recv.at[0])
    ns.meta[2] = dot_nn(ns.swap_a[...], ns.meta[1]).astype(BF16)
    start_all("dp", n_dp, n_table * cap, ns.meta.at[2], ns.meta.at[3], ns.send.at[1], ns.recv.at[1])

    for h in range(HEADS):
        attend_head(h, ns.act, ns.bias, ns.w, ns.dsl, ns.att)
    norm_att(ns.att, ns.ainv, ns.act, ns.gated)
    for half in range(2):
        ns.part[half] = dot_nn(ns.gated[...], ns.upstream[:, half * 256:half * 256 + 256])
    to_core = pltpu.make_async_remote_copy(
        src_ref=ns.part.at[1 - core],
        dst_ref=ns.other,
        send_sem=ns.send.at[2],
        recv_sem=ns.recv.at[2],
        device_id={"dp": dp + 1 - 2 * core},
        device_id_type=MESH,
    )
    to_core.start()
    att_backward(ns.w_out, ns.upstream, ns.att, ns.ainv, ns.act, ns.slope, ns.zg, ns.ag)
    to_core.wait_recv()
    ns.rs_send[...] = (ns.part[core] + ns.other[...]).astype(BF16)
    start_all("table", n_table, row_share, ns.rs_send, ns.rs_recv, ns.send.at[3], ns.recv.at[3])

    for h in range(HEADS):
        backward_head(h, ns.act, ns.ag, ns.w, ns.dsl, ns.ds, ns.slope, ns.zg)

    event_gradient(ns.w_in, ns.zg, ns.upstream, ns.xnt, ns.inv, ns.eg)
    first = (("table", n_table, n_dp * cap, ns.oh_a), ("dp", n_dp, n_table * cap, ns.oh_b))
    second = (("dp", n_dp, n_table * cap, ns.swap_a), ("table", n_table, n_dp * cap, ns.swap_b))
    for q in range(CHUNKS):
        axis, size, rows, oh = first[q % 2]
        ns.moved[q, 0] = dot_nt(oh[...], ns.eg[q * CW:q * CW + CW, :]).astype(BF16)
        start_all(axis, size, rows, ns.moved.at[q, 0], ns.moved.at[q, 1], ns.send.at[5 + q], ns.recv.at[5 + q])

    wait_bytes(ns.rs_recv, ns.recv.at[3])
    share = ns.rs_recv[0:row_share].astype(F32)
    for t in range(1, n_table):
        share = share + ns.rs_recv[t * row_share:(t + 1) * row_share].astype(F32)
    for g in range(2):
        ns.fin_send[g] = share[:, g * 128:g * 128 + 128]
    z = dp // 2
    for m in range(half_dp):
        target = core * half_dp + m
        group = ns.fin_send.at[m * col_share // 128]

        @pl.when(target == dp)
        def _():
            pltpu.make_async_copy(group, ns.fin_recv.at[z], ns.recv.at[4]).start()

        @pl.when(target != dp)
        def _():
            pltpu.make_async_remote_copy(
                src_ref=group,
                dst_ref=ns.fin_recv.at[z],
                send_sem=ns.fin_sem.at[m],
                recv_sem=ns.recv.at[4],
                device_id={"dp": target},
                device_id_type=MESH,
            ).start()

    wait_bytes(ns.meta.at[3], ns.recv.at[1])
    build_hits(ns.meta[3], ns.hits_a)
    build_hits(dot_nn(ns.swap_b[...], ns.meta[3]), ns.hits_b)

    for q in range(CHUNKS):
        axis, size, rows, swap = second[q % 2]
        wait_bytes(ns.moved.at[q, 1], ns.recv.at[5 + q])
        ns.moved[q, 2] = dot_nn(swap[...], ns.moved[q, 1]).astype(BF16)
        start_all(axis, size, rows, ns.moved.at[q, 2], ns.moved.at[q, 3], ns.send.at[9 + q], ns.recv.at[9 + q])

    wait_bytes(ns.fin_recv, ns.recv.at[4])
    total = ns.fin_recv[0]
    for k in range(1, half_dp):
        total = total + ns.fin_recv[k]
    lane = lax.rem(lax.rem(dp, half_dp) * col_share, 128)
    block = total[:, 0:col_share]
    for at in range(col_share, 128, col_share):
        block = jnp.where(lane == at, total[:, at:at + col_share], block)
    ns.out_grad[...] = block

    for q in range(CHUNKS):
        wait_bytes(ns.moved.at[q, 3], ns.recv.at[9 + q])
        hits = (ns.hits_a, ns.hits_b)[q % 2]
        ns.table_grad[:, q * CW:q * CW + CW] = dot_nn(hits[...], ns.moved[q, 3]).astype(BF16)

    by_table, by_dp = pl.ds(0, (n_table - 1) * n_dp * cap), pl.ds(0, (n_dp - 1) * n_table * cap)
    wait_bytes(ns.meta.at[0, by_table], ns.send.at[0])
    wait_bytes(ns.meta.at[2, by_dp], ns.send.at[1])
    to_core.wait_send()
    wait_bytes(ns.rs_send.at[pl.ds(0, (n_table - 1) * row_share)], ns.send.at[3])
    for m in range(half_dp):
        target = core * half_dp + m

        @pl.when(target != dp)
        def _():
            wait_bytes(ns.fin_send.at[m * col_share // 128], ns.fin_sem.at[m])
    for q in range(CHUNKS):
        one, two = (by_table, by_dp) if q % 2 == 0 else (by_dp, by_table)
        wait_bytes(ns.moved.at[q, 0, one], ns.send.at[5 + q])
        wait_bytes(ns.moved.at[q, 2, two], ns.send.at[9 + q])


INPUTS = ("events", "upstream", "w_in", "w_out", "lengths", "owners", "items")
OUTPUTS = ("out_grad", "table_grad")


def scratch(n_dp, n_table):
    row_share = D // n_table
    vmem = pltpu.VMEM
    return dict(
        bias=vmem((TOK, TOK), F32),
        xnt=vmem((D, TOK), F32),
        normedt=vmem((D, TOK), BF16),
        inv=vmem((1, TOK), F32),
        slope=vmem((4 * D, TOK), F32),
        act=vmem((4 * D, TOK), BF16),
        w=vmem((HEADS, TOK, TOK), BF16),
        dsl=vmem((HEADS, TOK, TOK), F32),
        att=vmem((D, TOK), F32),
        ainv=vmem((1, TOK), F32),
        gated=vmem((D, TOK), BF16),
        zg=vmem((4 * D, TOK), BF16),
        ag=vmem((D, TOK), BF16),
        ds=vmem((TOK, TOK), BF16),
        eg=vmem((D, TOK), BF16),
        oh_a=vmem((SLOTS, TOK), BF16),
        oh_b=vmem((SLOTS, TOK), BF16),
        swap_a=vmem((SLOTS, SLOTS), BF16),
        swap_b=vmem((SLOTS, SLOTS), BF16),
        hits_a=vmem((ROWS_DEV, SLOTS), BF16),
        hits_b=vmem((ROWS_DEV, SLOTS), BF16),
        meta=vmem((4, SLOTS, 128), BF16),
        moved=vmem((CHUNKS, 4, SLOTS, CW), BF16),
        part=vmem((2, D, 256), F32),
        other=vmem((D, 256), F32),
        rs_send=vmem((D, 256), BF16),
        rs_recv=vmem((D, 256), BF16),
        fin_send=vmem((2, row_share, 128), F32),
        fin_recv=vmem((n_dp // 2, row_share, 128), F32),
        send=pltpu.SemaphoreType.DMA((5 + 2 * CHUNKS,)),
        recv=pltpu.SemaphoreType.DMA((5 + 2 * CHUNKS,)),
        fin_sem=pltpu.SemaphoreType.DMA((n_dp // 2,)),
    )


def solution(mesh):
    n_dp, n_table = mesh.shape["dp"], mesh.shape["table"]
    in_vmem = pl.BlockSpec(memory_space=pltpu.VMEM)
    in_smem = pl.BlockSpec(memory_space=pltpu.SMEM)

    def local(events, upstream, w_in, w_out, lengths, owners, item_rows):
        return pl.pallas_call(
            functools.partial(kernel, n_dp, n_table),
            out_shape=(
                jax.ShapeDtypeStruct((D // n_table, D // n_dp), F32),
                jax.ShapeDtypeStruct((ROWS_DEV, D), BF16),
            ),
            in_specs=[in_vmem] * 4 + [in_smem] + [in_vmem] * 2,
            out_specs=(in_vmem, in_vmem),
            scratch_shapes=list(scratch(n_dp, n_table).values()),
            compiler_params=pltpu.CompilerParams(
                collective_id=0, has_side_effects=True, vmem_limit_bytes=60 << 20
            ),
        )(events, upstream, w_in, w_out, lengths, owners.reshape(1, TOK), item_rows.reshape(1, TOK))

    both = P(("dp", "table"), None)
    return jax.shard_map(
        local,
        mesh=mesh,
        in_specs=(both, both, P(), P(), both, both, P(("dp", "table"))),
        out_specs=(P("table", "dp"), both),
        check_vma=False,
    )
```

time: 414 us -> 76.4 us (0.18)
  waiting for transfers between devices: 263 us -> 0 us
  Pallas kernels: 0 us -> 72 us
  local copies, waits for them, and re-layouts: 46.6 us -> 3.56 us
  matrix products: 41.7 us -> 0 us
  starting transfers between devices: 37.6 us -> 0 us
  between operations: 14.2 us -> 0.64 us
  other arithmetic: 7.49 us -> 0 us
    reduce_scatter x1 -> x0, waiting for transfers between devices: 175 us -> none  [local(): lax.psum_scatter(lax.dot_general(gated, upstream, (((0,), (0,)), ((), ())...]
    pallas_call x0 -> x1, Pallas kernels: none -> 72 us  [local(): pl.pallas_call(functools.partial(kernel, n_dp, n_table), out_shape=(jax.S...]
    unnamed x3 -> x0, waiting for transfers between devices: 62 us -> none
    dot_general x11 -> x0, matrix products: 41.7 us -> none  [the longest x1 7.5 us: layer_grads(): jnp.einsum('qhd,khd->hqk', q_heads, k_heads, preferred_element_type=f32)]
    all_to_all x4 -> x0, starting transfers between devices: 37.5 us -> none  [the longest x1 13.8 us: local(): lax.all_to_all(moved_rows, 'dp', split_axis=0, concat_axis=0, tiled=True)]
    all_to_all x4 -> x0, waiting for transfers between devices: 26.2 us -> none  [the longest x1 22.1 us: local(): lax.all_to_all(send_data, 'table', split_axis=1, concat_axis=1, tiled=True)]
    reshape x9 -> x0, local copies, waits for them, and re-layouts: 17.1 us -> none  [the longest x2 5.58 us: local(): empty_data.at[slot].set(event_grad).reshape(n_dp, n_table, slots_cap, width)]
    unnamed x32 -> x2, local copies, waits for them, and re-layouts: 10.4 us -> 3.56 us
  transfers between devices with their start and end apart: 6 -> 0, of which waited for: 4 -> 0; matrix products, arithmetic and copies ran while one was open for 20% -> 0% of each run, Pallas kernels for 0% -> 0%
where the time goes in v1:
time: 76.4 us; the launch traced here: 76.2 us
  Pallas kernels  72 us (94%)
  local copies, waits for them, and re-layouts  3.56 us (5%)
    pallas_call x1, Pallas kernels, local(): pl.pallas_call(functools.partial(kernel, n_dp, n_table), out_shape=(jax.S...  72 us
    unnamed x2, local copies, waits for them, and re-layouts  3.56 us

profile of v1, /device:TPU:1, one launch (start us, length us, event | category | flops | bytes accessed | tf_op | source)
XLA Modules:
  0.0 76.2 jit_solution(9245850133981829346)
XLA Ops:
  0.6 72.0 %shard_map.86 = (f32[16,32]{1,0:T(8,128)}, bf16[1024,512]{1,0:T(8,128)(2,1)}) custom-call(bf16[512,512]{1,0:T(8,128)(2,1)} %refs_0_.1, bf16[512,512]{1,0:T(8,128)(2,1)} %refs_1_.1, bf16[512,2048]{1,0:T(8,128)(2,1)} %refs_2_.1, bf16[512,512]{1,0:T(8,128)(2,1)} %refs_3_.1, s32[1,8]{1,0:T(1,128)} %refs_4_.1, s32[1,512]{1,0:T(1,128)} %bitcast.2, s32[1,512]{1,0:T(1,128)} %bitcast.3), custom_call_target="tpu_custom_call" | custom-call | tf_op jit(solution)/shard_map/pallas_call | solution.py:417
  72.7 1.3 %copy.11 = f32[16,32]{1,0:T(8,128)} copy(f32[16,32]{1,0:T(8,128)} %get-tuple-element.4) | data formatting | bytes 4096
  74.0 2.3 %copy.12 = bf16[1024,512]{1,0:T(8,128)(2,1)} copy(bf16[1024,512]{1,0:T(8,128)(2,1)} %get-tuple-element.5) | data formatting | bytes 2097152

commit v2 on v1

--- a/solution.py
+++ b/solution.py
@@ -163,8 +163,6 @@
 MESH = pl.DeviceIdType.MESH
 SLOTS = 1024
 ROWS_DEV = 1024
-CHUNKS = 4
-CW = D // CHUNKS
 
 
 def log2(n):
@@ -176,8 +174,9 @@
     return jnp.where(at == cols_of, 1.0, 0.0).astype(BF16)
 
 
-def start_all(axis, size, rows, src_ref, dst_ref, send_sem, recv_sem):
-    me = lax.axis_index(axis)
+def start_all(axis, size, rows, src_ref, dst_ref, send_sem, recv_sem, lo=0, step=1):
+    at = lax.axis_index(axis)
+    me = lax.div(at - lo, step)
     mine = pl.ds(pl.multiple_of(me * rows, rows), rows)
     pltpu.make_async_copy(src_ref.at[mine], dst_ref.at[mine], recv_sem).start()
 
@@ -188,7 +187,7 @@
             dst_ref=dst_ref.at[mine],
             send_sem=send_sem,
             recv_sem=recv_sem,
-            device_id={axis: peer},
+            device_id={axis: lo + peer * step},
             device_id_type=MESH,
         ).start()
         return carry
@@ -201,7 +200,8 @@
 
 
 def route_slots(owner_ref, item_ref, n_dp, n_table, oh_a, oh_b, meta_ref):
-    cap = SLOTS // (n_dp * n_table)
+    pairs = n_dp * n_table
+    cap = SLOTS // pairs
     row = owner_ref[...]
     col = jnp.broadcast_to(row, (128, TOK)).T[:, 0:1]
     place_col = lax.broadcasted_iota(jnp.int32, (TOK, 1), 0)
@@ -213,34 +213,49 @@
     oh_b[...] = one_hot(SLOTS, dp * (n_table * cap) + table * cap + rank)
     code = item_ref[...] + 1
     line = lax.broadcasted_iota(jnp.int32, (128, TOK), 0)
-    high, low = (code >> 5).astype(F32), (code & 31).astype(F32)
-    meta_t = jnp.where(line == 0, high, jnp.where(line == 1, low, 0.0)).astype(BF16)
-    meta_ref[...] = dot_nt(oh_a[...], meta_t).astype(BF16)
-
-
-def build_swap(first, second, cap, ref):
-    out = lax.broadcasted_iota(jnp.int32, (SLOTS, 1), 0)
+    words = jnp.where((line & 1) == 0, code >> 5, code & 31).astype(F32)
+    meta_t = jnp.where((line >> 1) == rank, words, 0.0).astype(BF16)
+    meta_ref[...] = dot_nt(one_hot(pairs, table * n_dp + dp), meta_t).astype(BF16)
+
+
+def swap_rows(first, second, cap):
+    n = first * second * cap
+    out = lax.broadcasted_iota(jnp.int32, (n, 1), 0)
     slot = out & (cap - 1)
     a = (out >> log2(cap)) & (first - 1)
     b = out >> (log2(cap) + log2(first))
-    at = lax.broadcasted_iota(jnp.int32, (SLOTS, SLOTS), 1)
-    ref[...] = jnp.where(at == a * (second * cap) + b * cap + slot, 1.0, 0.0).astype(BF16)
-
-
-def build_hits(meta, ref):
-    lines = meta.astype(F32).T
-    item = (lines[0:1] * 32.0 + lines[1:2] - 1.0).astype(jnp.int32)
-    ref[...] = one_hot(ROWS_DEV, item)
+    at = lax.broadcasted_iota(jnp.int32, (n, n), 1)
+    return jnp.where(at == a * (second * cap) + b * cap + slot, 1.0, 0.0).astype(BF16)
+
+
+def item_lanes(meta, n_dp, n_table):
+    pairs = n_dp * n_table
+    cap = SLOTS // pairs
+    lines = meta.astype(F32).T.astype(BF16)
+    col = lax.broadcasted_iota(jnp.int32, (1, SLOTS), 1)
+    word = lax.broadcasted_iota(jnp.int32, (128, SLOTS), 0)
+    slot, pair = col & (cap - 1), col >> log2(cap)
+    other = (pair & (n_dp - 1)) * n_table + (pair >> log2(n_dp))
+    items = []
+    for order in (pair, other):
+        spread = dot_nn(lines, one_hot(pairs, order))
+        high = jnp.sum(jnp.where(word == 2 * slot, spread, 0.0), axis=0, keepdims=True)
+        low = jnp.sum(jnp.where(word == 2 * slot + 1, spread, 0.0), axis=0, keepdims=True)
+        items.append((high * 32.0 + low - 1.0).astype(jnp.int32))
+    return items
 
 
 def kernel(n_dp, n_table, *refs):
     names = INPUTS + OUTPUTS + tuple(scratch(n_dp, n_table))
-    r = dict(zip(names, refs))
-    ns = type("Refs", (), r)
+    ns = type("Refs", (), dict(zip(names, refs)))
     dp, table = lax.axis_index("dp"), lax.axis_index("table")
     core = lax.rem(dp, 2)
-    cap = SLOTS // (n_dp * n_table)
+    pairs = n_dp * n_table
+    cap = SLOTS // pairs
+    nx = 4
+    ny = n_table // nx
     row_share, col_share, half_dp = D // n_table, D // n_dp, n_dp // 2
+    x_rows = ny * row_share
 
     barrier = pltpu.get_barrier_semaphore()
     for axis, size, me in (("table", n_table, table), ("dp", n_dp, dp)):
@@ -251,27 +266,31 @@
             return carry
         lax.fori_loop(1, size, greet, 0)
 
+    loads = {}
+    for n, name in enumerate(("events", "w_in", "w_out", "upstream")):
+        loads[name] = pltpu.make_async_copy(getattr(ns, name), getattr(ns, name + "_v"), ns.load.at[n])
+        loads[name].start()
+
     route_slots(ns.owners, ns.items, n_dp, n_table, ns.oh_a, ns.oh_b, ns.meta.at[0])
-    pl.semaphore_wait(barrier, n_table + n_dp - 2)
-    start_all("table", n_table, n_dp * cap, ns.meta.at[0], ns.meta.at[1], ns.send.at[0], ns.recv.at[0])
-
     build_bias(ns.lengths, ns.bias)
     zero_corners(ns.w, (HEADS,))
     zero_corners(ns.ds, ())
-    build_swap(n_table, n_dp, cap, ns.swap_a)
-    build_swap(n_dp, n_table, cap, ns.swap_b)
-    normalize_events(ns.events, ns.xnt, ns.normedt, ns.inv)
-    project(ns.w_in, ns.normedt, ns.slope, ns.act)
-
-    wait_bytes(ns.meta.at[1], ns.recv.at[0])
-    ns.meta[2] = dot_nn(ns.swap_a[...], ns.meta[1]).astype(BF16)
-    start_all("dp", n_dp, n_table * cap, ns.meta.at[2], ns.meta.at[3], ns.send.at[1], ns.recv.at[1])
+    ns.swap_a[...] = swap_rows(n_table, n_dp, cap)
+    ns.swap_b[...] = swap_rows(n_dp, n_table, cap)
+    loads["events"].wait()
+    normalize_events(ns.events_v, ns.xnt, ns.normedt, ns.inv)
+    loads["w_in"].wait()
+    project(ns.w_in_v, ns.normedt, ns.slope, ns.act)
+
+    pl.semaphore_wait(barrier, n_table + n_dp - 2)
+    start_all("table", n_table, n_dp, ns.meta.at[0], ns.meta.at[1], ns.send.at[0], ns.recv.at[0])
 
     for h in range(HEADS):
         attend_head(h, ns.act, ns.bias, ns.w, ns.dsl, ns.att)
     norm_att(ns.att, ns.ainv, ns.act, ns.gated)
+    loads["upstream"].wait()
     for half in range(2):
-        ns.part[half] = dot_nn(ns.gated[...], ns.upstream[:, half * 256:half * 256 + 256])
+        ns.part[half] = dot_nn(ns.gated[...], ns.upstream_v[:, half * 256:half * 256 + 256])
     to_core = pltpu.make_async_remote_copy(
         src_ref=ns.part.at[1 - core],
         dst_ref=ns.other,
@@ -281,36 +300,66 @@
         device_id_type=MESH,
     )
     to_core.start()
-    att_backward(ns.w_out, ns.upstream, ns.att, ns.ainv, ns.act, ns.slope, ns.zg, ns.ag)
+    loads["w_out"].wait()
+    att_backward(ns.w_out_v, ns.upstream_v, ns.att, ns.ainv, ns.act, ns.slope, ns.zg, ns.ag)
+
+    def backward(lo, hi):
+        for h in range(lo, hi):
+            backward_head(h, ns.act, ns.ag, ns.w, ns.dsl, ns.ds, ns.slope, ns.zg)
+
+    backward(0, 2)
     to_core.wait_recv()
-    ns.rs_send[...] = (ns.part[core] + ns.other[...]).astype(BF16)
-    start_all("table", n_table, row_share, ns.rs_send, ns.rs_recv, ns.send.at[3], ns.recv.at[3])
-
-    for h in range(HEADS):
-        backward_head(h, ns.act, ns.ag, ns.w, ns.dsl, ns.ds, ns.slope, ns.zg)
-
-    event_gradient(ns.w_in, ns.zg, ns.upstream, ns.xnt, ns.inv, ns.eg)
-    first = (("table", n_table, n_dp * cap, ns.oh_a), ("dp", n_dp, n_table * cap, ns.oh_b))
-    second = (("dp", n_dp, n_table * cap, ns.swap_a), ("table", n_table, n_dp * cap, ns.swap_b))
-    for q in range(CHUNKS):
-        axis, size, rows, oh = first[q % 2]
-        ns.moved[q, 0] = dot_nt(oh[...], ns.eg[q * CW:q * CW + CW, :]).astype(BF16)
-        start_all(axis, size, rows, ns.moved.at[q, 0], ns.moved.at[q, 1], ns.send.at[5 + q], ns.recv.at[5 + q])
-
-    wait_bytes(ns.rs_recv, ns.recv.at[3])
-    share = ns.rs_recv[0:row_share].astype(F32)
-    for t in range(1, n_table):
-        share = share + ns.rs_recv[t * row_share:(t + 1) * row_share].astype(F32)
+    for t in range(n_table):
+        y, x = t // nx, t % nx
+        rows = slice(t * row_share, (t + 1) * row_share)
+        ns.x_send[x * x_rows + y * row_share:x * x_rows + (y + 1) * row_share] = (
+            ns.part[core, rows] + ns.other[rows]
+        ).astype(BF16)
+    start_all("table", nx, x_rows, ns.x_send, ns.x_recv, ns.send.at[3], ns.recv.at[3], lo=lax.div(table, nx) * nx)
+    wait_bytes(ns.meta.at[1], ns.recv.at[0])
+    ns.meta[2] = dot_nn(swap_rows(n_table, n_dp, 1), ns.meta[1]).astype(BF16)
+    start_all("dp", n_dp, n_table, ns.meta.at[2], ns.meta.at[3], ns.send.at[1], ns.recv.at[1])
+    backward(2, 7)
+    wait_bytes(ns.x_recv, ns.recv.at[3])
+    share = ns.x_recv[0:x_rows].astype(F32)
+    for x in range(1, nx):
+        share = share + ns.x_recv[x * x_rows:(x + 1) * x_rows].astype(F32)
+    ns.y_send[...] = share.astype(BF16)
+    start_all("table", ny, row_share, ns.y_send, ns.y_recv, ns.send.at[4], ns.recv.at[4], lo=lax.rem(table, nx), step=nx)
+    backward(7, 8)
+
+    event_gradient(ns.w_in_v, ns.zg, ns.upstream_v, ns.xnt, ns.inv, ns.eg)
+    first = (("table", n_table, n_dp * cap), ("dp", n_dp, n_table * cap))
+    second = first[::-1]
+
+    def hop_one(path, half):
+        lanes = pl.ds(half * 128, 128)
+        start_all(
+            *first[path], ns.moved.at[path, :, lanes], ns.landed.at[path, half],
+            ns.hop_send.at[path, half, 0], ns.hop_recv.at[path, half, 0],
+        )
+
+    ns.moved[0] = dot_nt(ns.oh_a[...], ns.eg[0:256, :]).astype(BF16)
+    hop_one(0, 0)
+    ns.moved[1] = dot_nt(ns.oh_b[...], ns.eg[256:512, :]).astype(BF16)
+    hop_one(1, 0)
+    hop_one(0, 1)
+    hop_one(1, 1)
+
+    wait_bytes(ns.y_recv, ns.recv.at[4])
+    share = ns.y_recv[0:row_share].astype(F32)
+    for y in range(1, ny):
+        share = share + ns.y_recv[y * row_share:(y + 1) * row_share].astype(F32)
     for g in range(2):
         ns.fin_send[g] = share[:, g * 128:g * 128 + 128]
-    z = dp // 2
+    z = lax.div(dp, 2)
     for m in range(half_dp):
         target = core * half_dp + m
         group = ns.fin_send.at[m * col_share // 128]
 
         @pl.when(target == dp)
         def _():
-            pltpu.make_async_copy(group, ns.fin_recv.at[z], ns.recv.at[4]).start()
+            pltpu.make_async_copy(group, ns.fin_recv.at[z], ns.recv.at[5]).start()
 
         @pl.when(target != dp)
         def _():
@@ -318,22 +367,26 @@
                 src_ref=group,
                 dst_ref=ns.fin_recv.at[z],
                 send_sem=ns.fin_sem.at[m],
-                recv_sem=ns.recv.at[4],
+                recv_sem=ns.recv.at[5],
                 device_id={"dp": target},
                 device_id_type=MESH,
             ).start()
 
     wait_bytes(ns.meta.at[3], ns.recv.at[1])
-    build_hits(ns.meta[3], ns.hits_a)
-    build_hits(dot_nn(ns.swap_b[...], ns.meta[3]), ns.hits_b)
-
-    for q in range(CHUNKS):
-        axis, size, rows, swap = second[q % 2]
-        wait_bytes(ns.moved.at[q, 1], ns.recv.at[5 + q])
-        ns.moved[q, 2] = dot_nn(swap[...], ns.moved[q, 1]).astype(BF16)
-        start_all(axis, size, rows, ns.moved.at[q, 2], ns.moved.at[q, 3], ns.send.at[9 + q], ns.recv.at[9 + q])
-
-    wait_bytes(ns.fin_recv, ns.recv.at[4])
+    items = item_lanes(ns.meta[3], n_dp, n_table)
+    ns.item_rows[0:1, :] = items[0]
+    ns.item_rows[1:2, :] = items[1]
+
+    for half in range(2):
+        for path, swap in ((0, ns.swap_a), (1, ns.swap_b)):
+            wait_bytes(ns.landed.at[path, half], ns.hop_recv.at[path, half, 0])
+            ns.again[path, half] = dot_nn(swap[...], ns.landed[path, half]).astype(BF16)
+            start_all(
+                *second[path], ns.again.at[path, half], ns.arrived.at[path, :, pl.ds(half * 128, 128)],
+                ns.hop_send.at[path, half, 1], ns.hop_recv.at[path, half, 1],
+            )
+
+    wait_bytes(ns.fin_recv, ns.recv.at[5])
     total = ns.fin_recv[0]
     for k in range(1, half_dp):
         total = total + ns.fin_recv[k]
@@ -341,38 +394,54 @@
     block = total[:, 0:col_share]
     for at in range(col_share, 128, col_share):
         block = jnp.where(lane == at, total[:, at:at + col_share], block)
-    ns.out_grad[...] = block
-
-    for q in range(CHUNKS):
-        wait_bytes(ns.moved.at[q, 3], ns.recv.at[9 + q])
-        hits = (ns.hits_a, ns.hits_b)[q % 2]
-        ns.table_grad[:, q * CW:q * CW + CW] = dot_nn(hits[...], ns.moved[q, 3]).astype(BF16)
-
-    by_table, by_dp = pl.ds(0, (n_table - 1) * n_dp * cap), pl.ds(0, (n_dp - 1) * n_table * cap)
-    wait_bytes(ns.meta.at[0, by_table], ns.send.at[0])
-    wait_bytes(ns.meta.at[2, by_dp], ns.send.at[1])
+    ns.grad_block[...] = block
+
+    wait_bytes(ns.meta.at[0, pl.ds(0, (n_table - 1) * n_dp)], ns.send.at[0])
+    wait_bytes(ns.meta.at[2, pl.ds(0, (n_dp - 1) * n_table)], ns.send.at[1])
     to_core.wait_send()
-    wait_bytes(ns.rs_send.at[pl.ds(0, (n_table - 1) * row_share)], ns.send.at[3])
+    wait_bytes(ns.x_send.at[pl.ds(0, (nx - 1) * x_rows)], ns.send.at[3])
+    if ny > 1:
+        wait_bytes(ns.y_send.at[pl.ds(0, (ny - 1) * row_share)], ns.send.at[4])
     for m in range(half_dp):
         target = core * half_dp + m
 
         @pl.when(target != dp)
         def _():
             wait_bytes(ns.fin_send.at[m * col_share // 128], ns.fin_sem.at[m])
-    for q in range(CHUNKS):
-        one, two = (by_table, by_dp) if q % 2 == 0 else (by_dp, by_table)
-        wait_bytes(ns.moved.at[q, 0, one], ns.send.at[5 + q])
-        wait_bytes(ns.moved.at[q, 2, two], ns.send.at[9 + q])
+    for half in range(2):
+        for path in range(2):
+            for hop, (_, size, rows) in enumerate((first[path], second[path])):
+                wait_bytes(ns.again.at[path, half, pl.ds(0, (size - 1) * rows)], ns.hop_send.at[path, half, hop])
+    for half in range(2):
+        for path in range(2):
+            wait_bytes(ns.arrived.at[path, :, pl.ds(half * 128, 128)], ns.hop_recv.at[path, half, 1])
+
+
+def place_kernel(arrived_ref, item_ref, block_ref, out_ref, table_ref, rows, load):
+    copies = [pltpu.make_async_copy(arrived_ref.at[p], rows.at[p], load.at[p]) for p in range(2)]
+    for copy in copies:
+        copy.start()
+    out_ref[...] = block_ref[...]
+    for p in range(2):
+        hits = one_hot(ROWS_DEV, item_ref[p:p + 1, :])
+        copies[p].wait()
+        table_ref[:, p * 256:p * 256 + 256] = dot_nn(hits, rows[p]).astype(BF16)
 
 
 INPUTS = ("events", "upstream", "w_in", "w_out", "lengths", "owners", "items")
-OUTPUTS = ("out_grad", "table_grad")
+OUTPUTS = ("grad_block", "item_rows", "arrived")
 
 
 def scratch(n_dp, n_table):
     row_share = D // n_table
+    pairs = n_dp * n_table
     vmem = pltpu.VMEM
+    dma = pltpu.SemaphoreType.DMA
     return dict(
+        events_v=vmem((TOK, D), BF16),
+        upstream_v=vmem((TOK, D), BF16),
+        w_in_v=vmem((D, 4 * D), BF16),
+        w_out_v=vmem((D, D), BF16),
         bias=vmem((TOK, TOK), F32),
         xnt=vmem((D, TOK), F32),
         normedt=vmem((D, TOK), BF16),
@@ -392,19 +461,24 @@
         oh_b=vmem((SLOTS, TOK), BF16),
         swap_a=vmem((SLOTS, SLOTS), BF16),
         swap_b=vmem((SLOTS, SLOTS), BF16),
-        hits_a=vmem((ROWS_DEV, SLOTS), BF16),
-        hits_b=vmem((ROWS_DEV, SLOTS), BF16),
-        meta=vmem((4, SLOTS, 128), BF16),
-        moved=vmem((CHUNKS, 4, SLOTS, CW), BF16),
+        meta=vmem((4, pairs, 128), BF16),
+        moved=vmem((2, SLOTS, 256), BF16),
+        landed=vmem((2, 2, SLOTS, 128), BF16),
+        again=vmem((2, 2, SLOTS, 128), BF16),
         part=vmem((2, D, 256), F32),
         other=vmem((D, 256), F32),
-        rs_send=vmem((D, 256), BF16),
-        rs_recv=vmem((D, 256), BF16),
+        x_send=vmem((D, 256), BF16),
+        x_recv=vmem((D, 256), BF16),
+        y_send=vmem((D // 4, 256), BF16),
+        y_recv=vmem((D // 4, 256), BF16),
         fin_send=vmem((2, row_share, 128), F32),
         fin_recv=vmem((n_dp // 2, row_share, 128), F32),
-        send=pltpu.SemaphoreType.DMA((5 + 2 * CHUNKS,)),
-        recv=pltpu.SemaphoreType.DMA((5 + 2 * CHUNKS,)),
-        fin_sem=pltpu.SemaphoreType.DMA((n_dp // 2,)),
+        load=dma((4,)),
+        send=dma((6,)),
+        recv=dma((6,)),
+        hop_send=dma((2, 2, 2)),
+        hop_recv=dma((2, 2, 2)),
+        fin_sem=dma((n_dp // 2,)),
     )
 
 
@@ -412,21 +486,32 @@
     n_dp, n_table = mesh.shape["dp"], mesh.shape["table"]
     in_vmem = pl.BlockSpec(memory_space=pltpu.VMEM)
     in_smem = pl.BlockSpec(memory_space=pltpu.SMEM)
+    anywhere = pl.BlockSpec(memory_space=pl.ANY)
 
     def local(events, upstream, w_in, w_out, lengths, owners, item_rows):
-        return pl.pallas_call(
+        block = jax.ShapeDtypeStruct((D // n_table, D // n_dp), F32)
+        grad_block, items, arrived = pl.pallas_call(
             functools.partial(kernel, n_dp, n_table),
             out_shape=(
-                jax.ShapeDtypeStruct((D // n_table, D // n_dp), F32),
-                jax.ShapeDtypeStruct((ROWS_DEV, D), BF16),
+                block,
+                jax.ShapeDtypeStruct((8, SLOTS), jnp.int32),
+                jax.ShapeDtypeStruct((2, SLOTS, 256), BF16),
             ),
-            in_specs=[in_vmem] * 4 + [in_smem] + [in_vmem] * 2,
-            out_specs=(in_vmem, in_vmem),
+            in_specs=[anywhere] * 4 + [in_smem] + [in_vmem] * 2,
+            out_specs=(in_vmem, in_vmem, anywhere),
             scratch_shapes=list(scratch(n_dp, n_table).values()),
             compiler_params=pltpu.CompilerParams(
                 collective_id=0, has_side_effects=True, vmem_limit_bytes=60 << 20
             ),
         )(events, upstream, w_in, w_out, lengths, owners.reshape(1, TOK), item_rows.reshape(1, TOK))
+        return pl.pallas_call(
+            place_kernel,
+            out_shape=(block, jax.ShapeDtypeStruct((ROWS_DEV, D), BF16)),
+            in_specs=[anywhere, in_vmem, in_vmem],
+            out_specs=(in_vmem, in_vmem),
+            scratch_shapes=[pltpu.VMEM((2, SLOTS, 256), BF16), pltpu.SemaphoreType.DMA((2,))],
+            compiler_params=pltpu.CompilerParams(vmem_limit_bytes=60 << 20),
+        )(arrived, items, grad_block)
 
     both = P(("dp", "table"), None)
     return jax.shard_map(

time: 76.4 us -> 69 us (0.903)
  Pallas kernels: 72 us -> 68 us
  local copies, waits for them, and re-layouts: 3.56 us -> 0 us
    pallas_call x1 -> x2, Pallas kernels: 72 us -> 68 us  [the longest x1 62.3 us: local(): pl.pallas_call(functools.partial(kernel, n_dp, n_table), out_shape=(block...]
    unnamed x2 -> x0, local copies, waits for them, and re-layouts: 3.56 us -> none
where the time goes in v2:
time: 69 us; the launch traced here: 68.8 us
  Pallas kernels  68 us (99%)
  between operations  0.8 us (1%)
    pallas_call x1, Pallas kernels, local(): pl.pallas_call(functools.partial(kernel, n_dp, n_table), out_shape=(block...  62.3 us
    pallas_call x1, Pallas kernels, local(): pl.pallas_call(place_kernel, out_shape=(block, jax.ShapeDtypeStruct((ROWS...  5.65 us

profile of v2, /device:TPU:1, one launch (start us, length us, event | category | flops | bytes accessed | tf_op | source)
XLA Modules:
  0.0 68.8 jit_solution(7364506271061275896)
XLA Ops:
  0.6 62.3 %shard_map.86 = (f32[16,32]{1,0:T(8,128)}, s32[8,1024]{1,0:T(8,128)}, bf16[2,1024,256]{2,1,0:T(8,128)(2,1)}) custom-call(bf16[512,512]{1,0:T(8,128)(2,1)} %refs_0_.1, bf16[512,512]{1,0:T(8,128)(2,1)} %refs_1_.1, bf16[512,2048]{1,0:T(8,128)(2,1)} %refs_2_.1, bf16[512,512]{1,0:T(8,128)(2,1)} %refs_3_.1, s32[1,8]{1,0:T(1,128)} %refs_4_.1, s32[1,512]{1,0:T(1,128)} %bitcast.2, ...), custom_call_target="tpu_custom_call" | custom-call | tf_op jit(solution)/shard_map/pallas_call | solution.py:493
  63.0 5.7 %shard_map.87 = (f32[16,32]{1,0:T(8,128)}, bf16[1024,512]{1,0:T(8,128)(2,1)}) custom-call(bf16[2,1024,256]{2,1,0:T(8,128)(2,1)} %get-tuple-element.5.arrived_ref, s32[8,1024]{1,0:T(8,128)} %get-tuple-element.6.item_ref, f32[16,32]{1,0:T(8,128)} %get-tuple-element.7.block_ref), custom_call_target="tpu_custom_call" | custom-call | tf_op jit(solution)/shard_map/pallas_call | solution.py:507

commit v3 on v2

--- a/solution.py
+++ b/solution.py
@@ -67,11 +67,12 @@
     inv_ref[...] = inv
 
 
-def project(w_in_ref, normedt_ref, slope_ref, act_ref):
+def project(w_in_ref, normedt_ref, slope_ref, act_ref, half_ref):
     for c in range(16):
         lo = c * 128
-        wt = w_in_ref[:, lo:lo + 128].T
+        wt = w_in_ref[0:D, lo:lo + 128].T
         half = dot_nn(wt, normedt_ref[...]) * 0.5
+        half_ref[lo:lo + 128, :] = half
         t = jnp.tanh(half)
         p = 1.0 + t
         act = half * p
@@ -117,52 +118,67 @@
     gated_ref[...] = (an * act_ref[0:512, :].astype(F32)).astype(BF16)
 
 
-def att_backward(w_out_ref, up_ref, att_ref, ainv_ref, act_ref, slope_ref, zg_ref, ag_ref):
-    gg = dot_nt(w_out_ref[...], up_ref[...])
+def put_z_grad(at, lanes, joined, slope_ref, half_ref, zg_ref, dot_ref):
+    grad = (joined * slope_ref[at, lanes]).astype(BF16)
+    zg_ref[at, lanes] = grad
+    dot_ref[:, lanes] += jnp.sum(grad.astype(F32) * half_ref[at, lanes], axis=0, keepdims=True)
+
+
+def att_backward(w_out_ref, up_ref, upt_ref, att_ref, ainv_ref, act_ref, ag_ref, z_refs):
+    upt_ref[...] = up_ref[...].T
+    gg = dot_nn(w_out_ref[...], upt_ref[...])
     an = att_ref[...]
-    zg_ref[0:512, :] = (gg * an * slope_ref[0:512, :]).astype(BF16)
+    put_z_grad(slice(0, 512), slice(0, 512), gg * an, *z_refs)
     g = gg * act_ref[0:512, :].astype(F32)
     first = jnp.mean(g, axis=0, keepdims=True)
     second = jnp.mean(g * an, axis=0, keepdims=True)
     ag_ref[...] = ((g - first - an * second) * (ainv_ref[...] * (1.0 / 128.0))).astype(BF16)
 
 
-def backward_head(h, act_ref, ag_ref, w_ref, dsl_ref, ds_ref, slope_ref, zg_ref):
-    r = pl.multiple_of(h * HD, HD)
-    qt = act_ref[pl.ds(1024 + r, HD), :]
-    kt = act_ref[pl.ds(1536 + r, HD), :]
-    v = act_ref[pl.ds(512 + r, HD), :].T
-    ag = ag_ref[pl.ds(r, HD), :]
+def backward_head(h, act_ref, ag_ref, w_ref, dsl_ref, ds_ref, z_refs):
+    r = h * HD
+    qt = act_ref[1024 + r:1024 + r + HD, :]
+    kt = act_ref[1536 + r:1536 + r + HD, :]
+    v = act_ref[512 + r:512 + r + HD, :].T
+    ag = ag_ref[r:r + HD, :]
     for jb in range(TOK // JB):
         lo, hi = window(jb)
         wg = dot_nn(v[lo:lo + JB], ag[:, lo:hi])
         ds_ref[lo:lo + JB, lo:hi] = (wg * dsl_ref[h, lo:lo + JB, lo:hi]).astype(BF16)
-    vg0 = dot_nt(ag, w_ref[h, 0:256, :])
-    vg1 = dot_nt(ag[:, 256:512], w_ref[h, 256:512, 256:512])
-    zg_ref[pl.ds(512 + r, HD), 0:256] = (vg0 * 2.0 * slope_ref[pl.ds(512 + r, HD), 0:256]).astype(BF16)
-    zg_ref[pl.ds(512 + r, HD), 256:512] = (vg1 * 2.0 * slope_ref[pl.ds(512 + r, HD), 256:512]).astype(BF16)
-    qg0 = dot_nn(kt[:, 0:256], ds_ref[0:256, 0:256])
-    qg1 = dot_nn(kt, ds_ref[:, 256:512])
-    zg_ref[pl.ds(1024 + r, HD), 0:256] = (qg0 * 0.125 * slope_ref[pl.ds(1024 + r, HD), 0:256]).astype(BF16)
-    zg_ref[pl.ds(1024 + r, HD), 256:512] = (qg1 * 0.125 * slope_ref[pl.ds(1024 + r, HD), 256:512]).astype(BF16)
-    kg0 = dot_nt(qt, ds_ref[0:256, :])
-    kg1 = dot_nt(qt[:, 256:512], ds_ref[256:512, 256:512])
-    zg_ref[pl.ds(1536 + r, HD), 0:256] = (kg0 * 0.125 * slope_ref[pl.ds(1536 + r, HD), 0:256]).astype(BF16)
-    zg_ref[pl.ds(1536 + r, HD), 256:512] = (kg1 * 0.125 * slope_ref[pl.ds(1536 + r, HD), 256:512]).astype(BF16)
-
-
-def event_gradient(w_in_ref, zg_ref, up_ref, xnt_ref, inv_ref, eg_ref):
-    ng = dot_nn(w_in_ref[...], zg_ref[...])
-    xn = xnt_ref[...]
-    first = jnp.mean(ng, axis=0, keepdims=True)
-    second = jnp.mean(ng * xn, axis=0, keepdims=True)
-    back = (ng - first - xn * second) * (inv_ref[...] * 0.5)
-    eg_ref[...] = (up_ref[...].T.astype(F32) + back).astype(BF16)
+    left, right = slice(0, 256), slice(256, 512)
+    rows = [slice(base + r, base + r + HD) for base in (512, 1024, 1536)]
+    put_z_grad(rows[0], left, dot_nt(ag, w_ref[h, 0:256, :]) * 2.0, *z_refs)
+    put_z_grad(rows[0], right, dot_nt(ag[:, right], w_ref[h, right, right]) * 2.0, *z_refs)
+    put_z_grad(rows[1], left, dot_nn(kt[:, left], ds_ref[left, left]) * 0.125, *z_refs)
+    put_z_grad(rows[1], right, dot_nn(kt, ds_ref[:, right]) * 0.125, *z_refs)
+    put_z_grad(rows[2], left, dot_nt(qt, ds_ref[left, :]) * 0.125, *z_refs)
+    put_z_grad(rows[2], right, dot_nt(qt[:, right], ds_ref[right, right]) * 0.125, *z_refs)
+
+
+def sum_rows(w_in_ref):
+    sums = dot_nn(jnp.ones((8, D), BF16), w_in_ref[0:D, :])
+    high = sums.astype(BF16)
+    w_in_ref[D:D + 16, :] = jnp.concatenate([high, (sums - high.astype(F32)).astype(BF16)], axis=0)
+
+
+def event_gradient(path, w_in_ref, zg_ref, dot_ref, stat_ref, upt_ref, xnt_ref, inv_ref):
+    if path == 0:
+        ng = dot_nn(w_in_ref[256:D + 16, :], zg_ref[...])
+        stat_ref[0:1, :] = (ng[256:257] + ng[264:265]) * (1.0 / 512.0)
+        stat_ref[1:2, :] = dot_ref[...] * (1.0 / 256.0)
+        ng = ng[0:256]
+        at = slice(256, 512)
+    else:
+        at = slice(0, 256)
+        ng = dot_nn(w_in_ref[at, :], zg_ref[...])
+    back = (ng - stat_ref[0:1, :] - xnt_ref[at, :] * stat_ref[1:2, :]) * (inv_ref[...] * 0.5)
+    return (upt_ref[at, :].astype(F32) + back).astype(BF16)
 
 
 MESH = pl.DeviceIdType.MESH
 SLOTS = 1024
 ROWS_DEV = 1024
+PLACE_BLOCKS = 4
 
 
 def log2(n):
@@ -268,22 +284,20 @@
 
     loads = {}
     for n, name in enumerate(("events", "w_in", "w_out", "upstream")):
-        loads[name] = pltpu.make_async_copy(getattr(ns, name), getattr(ns, name + "_v"), ns.load.at[n])
+        held = getattr(ns, name + "_v")
+        held = held.at[pl.ds(0, D)] if name == "w_in" else held
+        loads[name] = pltpu.make_async_copy(getattr(ns, name), held, ns.load.at[n])
         loads[name].start()
 
     route_slots(ns.owners, ns.items, n_dp, n_table, ns.oh_a, ns.oh_b, ns.meta.at[0])
     build_bias(ns.lengths, ns.bias)
     zero_corners(ns.w, (HEADS,))
     zero_corners(ns.ds, ())
-    ns.swap_a[...] = swap_rows(n_table, n_dp, cap)
-    ns.swap_b[...] = swap_rows(n_dp, n_table, cap)
     loads["events"].wait()
     normalize_events(ns.events_v, ns.xnt, ns.normedt, ns.inv)
     loads["w_in"].wait()
-    project(ns.w_in_v, ns.normedt, ns.slope, ns.act)
-
-    pl.semaphore_wait(barrier, n_table + n_dp - 2)
-    start_all("table", n_table, n_dp, ns.meta.at[0], ns.meta.at[1], ns.send.at[0], ns.recv.at[0])
+    project(ns.w_in_v, ns.normedt, ns.slope, ns.act, ns.half)
+    sum_rows(ns.w_in_v)
 
     for h in range(HEADS):
         attend_head(h, ns.act, ns.bias, ns.w, ns.dsl, ns.att)
@@ -291,6 +305,8 @@
     loads["upstream"].wait()
     for half in range(2):
         ns.part[half] = dot_nn(ns.gated[...], ns.upstream_v[:, half * 256:half * 256 + 256])
+    pl.semaphore_wait(barrier, n_table + n_dp - 2)
+    start_all("table", n_table, n_dp, ns.meta.at[0], ns.meta.at[1], ns.send.at[0], ns.recv.at[0])
     to_core = pltpu.make_async_remote_copy(
         src_ref=ns.part.at[1 - core],
         dst_ref=ns.other,
@@ -301,13 +317,38 @@
     )
     to_core.start()
     loads["w_out"].wait()
-    att_backward(ns.w_out_v, ns.upstream_v, ns.att, ns.ainv, ns.act, ns.slope, ns.zg, ns.ag)
-
-    def backward(lo, hi):
-        for h in range(lo, hi):
-            backward_head(h, ns.act, ns.ag, ns.w, ns.dsl, ns.ds, ns.slope, ns.zg)
-
-    backward(0, 2)
+    ns.dot[...] = jnp.zeros_like(ns.dot)
+    z_refs = (ns.slope, ns.half, ns.zg, ns.dot)
+    att_backward(ns.w_out_v, ns.upstream_v, ns.upt, ns.att, ns.ainv, ns.act, ns.ag, z_refs)
+    for h in range(HEADS):
+        backward_head(h, ns.act, ns.ag, ns.w, ns.dsl, ns.ds, z_refs)
+
+    first = (("table", n_table, n_dp * cap), ("dp", n_dp, n_table * cap))
+    second = first[::-1]
+
+    def hop_one(path, half):
+        lanes = pl.ds(half * 128, 128)
+        start_all(
+            *first[path], ns.moved.at[path, :, lanes], ns.landed.at[path, half],
+            ns.hop_send.at[path, half, 0], ns.hop_recv.at[path, half, 0],
+        )
+
+    def hop_two(path, half):
+        swap = (ns.swap_a, ns.swap_b)[path]
+        wait_bytes(ns.landed.at[path, half], ns.hop_recv.at[path, half, 0])
+        ns.again[path, half] = dot_nn(swap[...], ns.landed[path, half]).astype(BF16)
+        start_all(
+            *second[path], ns.again.at[path, half], ns.arrived.at[path, :, pl.ds(half * 128, 128)],
+            ns.hop_send.at[path, half, 1], ns.hop_recv.at[path, half, 1],
+        )
+
+    for path, slots in ((0, ns.oh_a), (1, ns.oh_b)):
+        grad = event_gradient(path, ns.w_in_v, ns.zg, ns.dot, ns.stat, ns.upt, ns.xnt, ns.inv)
+        ns.moved[path] = dot_nt(slots[...], grad).astype(BF16)
+        hop_one(path, 0)
+    hop_one(0, 1)
+    hop_one(1, 1)
+
     to_core.wait_recv()
     for t in range(n_table):
         y, x = t // nx, t % nx
@@ -319,32 +360,18 @@
     wait_bytes(ns.meta.at[1], ns.recv.at[0])
     ns.meta[2] = dot_nn(swap_rows(n_table, n_dp, 1), ns.meta[1]).astype(BF16)
     start_all("dp", n_dp, n_table, ns.meta.at[2], ns.meta.at[3], ns.send.at[1], ns.recv.at[1])
-    backward(2, 7)
+    ns.swap_a[...] = swap_rows(n_table, n_dp, cap)
+    ns.swap_b[...] = swap_rows(n_dp, n_table, cap)
+
     wait_bytes(ns.x_recv, ns.recv.at[3])
     share = ns.x_recv[0:x_rows].astype(F32)
     for x in range(1, nx):
         share = share + ns.x_recv[x * x_rows:(x + 1) * x_rows].astype(F32)
     ns.y_send[...] = share.astype(BF16)
     start_all("table", ny, row_share, ns.y_send, ns.y_recv, ns.send.at[4], ns.recv.at[4], lo=lax.rem(table, nx), step=nx)
-    backward(7, 8)
-
-    event_gradient(ns.w_in_v, ns.zg, ns.upstream_v, ns.xnt, ns.inv, ns.eg)
-    first = (("table", n_table, n_dp * cap), ("dp", n_dp, n_table * cap))
-    second = first[::-1]
-
-    def hop_one(path, half):
-        lanes = pl.ds(half * 128, 128)
-        start_all(
-            *first[path], ns.moved.at[path, :, lanes], ns.landed.at[path, half],
-            ns.hop_send.at[path, half, 0], ns.hop_recv.at[path, half, 0],
-        )
-
-    ns.moved[0] = dot_nt(ns.oh_a[...], ns.eg[0:256, :]).astype(BF16)
-    hop_one(0, 0)
-    ns.moved[1] = dot_nt(ns.oh_b[...], ns.eg[256:512, :]).astype(BF16)
-    hop_one(1, 0)
-    hop_one(0, 1)
-    hop_one(1, 1)
+
+    hop_two(0, 0)
+    hop_two(1, 0)
 
     wait_bytes(ns.y_recv, ns.recv.at[4])
     share = ns.y_recv[0:row_share].astype(F32)
@@ -377,14 +404,8 @@
     ns.item_rows[0:1, :] = items[0]
     ns.item_rows[1:2, :] = items[1]
 
-    for half in range(2):
-        for path, swap in ((0, ns.swap_a), (1, ns.swap_b)):
-            wait_bytes(ns.landed.at[path, half], ns.hop_recv.at[path, half, 0])
-            ns.again[path, half] = dot_nn(swap[...], ns.landed[path, half]).astype(BF16)
-            start_all(
-                *second[path], ns.again.at[path, half], ns.arrived.at[path, :, pl.ds(half * 128, 128)],
-                ns.hop_send.at[path, half, 1], ns.hop_recv.at[path, half, 1],
-            )
+    hop_two(0, 1)
+    hop_two(1, 1)
 
     wait_bytes(ns.fin_recv, ns.recv.at[5])
     total = ns.fin_recv[0]
@@ -417,15 +438,24 @@
             wait_bytes(ns.arrived.at[path, :, pl.ds(half * 128, 128)], ns.hop_recv.at[path, half, 1])
 
 
-def place_kernel(arrived_ref, item_ref, block_ref, out_ref, table_ref, rows, load):
+def place_kernel(arrived_ref, item_ref, block_ref, out_ref, table_ref, rows, built, load, store):
     copies = [pltpu.make_async_copy(arrived_ref.at[p], rows.at[p], load.at[p]) for p in range(2)]
     for copy in copies:
         copy.start()
     out_ref[...] = block_ref[...]
-    for p in range(2):
-        hits = one_hot(ROWS_DEV, item_ref[p:p + 1, :])
-        copies[p].wait()
-        table_ref[:, p * 256:p * 256 + 256] = dot_nn(hits, rows[p]).astype(BF16)
+    blocks = built.shape[0]
+    size = ROWS_DEV // blocks
+    stores = []
+    for b in range(blocks):
+        for p in range(2):
+            hits = one_hot(size, item_ref[p:p + 1, :] - b * size)
+            if b == 0:
+                copies[p].wait()
+            built[b, :, 256 - p * 256:512 - p * 256] = dot_nn(hits, rows[p]).astype(BF16)
+        stores.append(pltpu.make_async_copy(built.at[b], table_ref.at[pl.ds(b * size, size)], store.at[b]))
+        stores[-1].start()
+    for copy in stores:
+        copy.wait()
 
 
 INPUTS = ("events", "upstream", "w_in", "w_out", "lengths", "owners", "items")
@@ -440,7 +470,11 @@
     return dict(
         events_v=vmem((TOK, D), BF16),
         upstream_v=vmem((TOK, D), BF16),
-        w_in_v=vmem((D, 4 * D), BF16),
+        w_in_v=vmem((D + 16, 4 * D), BF16),
+        half=vmem((4 * D, TOK), F32),
+        upt=vmem((D, TOK), BF16),
+        dot=vmem((1, TOK), F32),
+        stat=vmem((8, TOK), F32),
         w_out_v=vmem((D, D), BF16),
         bias=vmem((TOK, TOK), F32),
         xnt=vmem((D, TOK), F32),
@@ -456,7 +490,6 @@
         zg=vmem((4 * D, TOK), BF16),
         ag=vmem((D, TOK), BF16),
         ds=vmem((TOK, TOK), BF16),
-        eg=vmem((D, TOK), BF16),
         oh_a=vmem((SLOTS, TOK), BF16),
         oh_b=vmem((SLOTS, TOK), BF16),
         swap_a=vmem((SLOTS, SLOTS), BF16),
@@ -508,8 +541,13 @@
             place_kernel,
             out_shape=(block, jax.ShapeDtypeStruct((ROWS_DEV, D), BF16)),
             in_specs=[anywhere, in_vmem, in_vmem],
-            out_specs=(in_vmem, in_vmem),
-            scratch_shapes=[pltpu.VMEM((2, SLOTS, 256), BF16), pltpu.SemaphoreType.DMA((2,))],
+            out_specs=(in_vmem, anywhere),
+            scratch_shapes=[
+                pltpu.VMEM((2, SLOTS, 256), BF16),
+                pltpu.VMEM((PLACE_BLOCKS, ROWS_DEV // PLACE_BLOCKS, D), BF16),
+                pltpu.SemaphoreType.DMA((2,)),
+                pltpu.SemaphoreType.DMA((PLACE_BLOCKS,)),
+            ],
             compiler_params=pltpu.CompilerParams(vmem_limit_bytes=60 << 20),
         )(arrived, items, grad_block)
 

time: 69 us -> 66.4 us (0.962)
  Pallas kernels: 68 us -> 65.3 us
    pallas_call x1, Pallas kernels: 62.3 us -> 60.4 us  [local(): pl.pallas_call(functools.partial(kernel, n_dp, n_table), out_shape=(block...]
    pallas_call x1, Pallas kernels: 5.65 us -> 4.92 us  [local(): pl.pallas_call(place_kernel, out_shape=(block, jax.ShapeDtypeStruct((ROWS...]
where the time goes in v3:
time: 66.4 us; the launch traced here: 66.1 us
  Pallas kernels  65.3 us (98%)
  between operations  0.8 us (1%)
    pallas_call x1, Pallas kernels, local(): pl.pallas_call(functools.partial(kernel, n_dp, n_table), out_shape=(block...  60.4 us
    pallas_call x1, Pallas kernels, local(): pl.pallas_call(place_kernel, out_shape=(block, jax.ShapeDtypeStruct((ROWS...  4.92 us

profile of v3, /device:TPU:1, one launch (start us, length us, event | category | flops | bytes accessed | tf_op | source)
XLA Modules:
  0.0 66.1 jit_solution(17912212423352967966)
XLA Ops:
  0.6 60.4 %shard_map.86 = (f32[16,32]{1,0:T(8,128)}, s32[8,1024]{1,0:T(8,128)}, bf16[2,1024,256]{2,1,0:T(8,128)(2,1)}) custom-call(bf16[512,512]{1,0:T(8,128)(2,1)} %refs_0_.1, bf16[512,512]{1,0:T(8,128)(2,1)} %refs_1_.1, bf16[512,2048]{1,0:T(8,128)(2,1)} %refs_2_.1, bf16[512,512]{1,0:T(8,128)(2,1)} %refs_3_.1, s32[1,8]{1,0:T(1,128)} %refs_4_.1, s32[1,512]{1,0:T(1,128)} %bitcast.2, ...), custom_call_target="tpu_custom_call" | custom-call | tf_op jit(solution)/shard_map/pallas_call | solution.py:526
  61.1 4.9 %shard_map.87 = (f32[16,32]{1,0:T(8,128)}, bf16[1024,512]{1,0:T(8,128)(2,1)}) custom-call(bf16[2,1024,256]{2,1,0:T(8,128)(2,1)} %get-tuple-element.5.arrived_ref, s32[8,1024]{1,0:T(8,128)} %get-tuple-element.6.item_ref, f32[16,32]{1,0:T(8,128)} %get-tuple-element.7.block_ref), custom_call_target="tpu_custom_call" | custom-call | tf_op jit(solution)/shard_map/pallas_call | solution.py:540

commit v4 on v3

--- a/solution.py
+++ b/solution.py
@@ -322,6 +322,15 @@
     att_backward(ns.w_out_v, ns.upstream_v, ns.upt, ns.att, ns.ainv, ns.act, ns.ag, z_refs)
     for h in range(HEADS):
         backward_head(h, ns.act, ns.ag, ns.w, ns.dsl, ns.ds, z_refs)
+        if h == 5:
+            to_core.wait_recv()
+            for t in range(n_table):
+                y, x = t // nx, t % nx
+                rows = slice(t * row_share, (t + 1) * row_share)
+                ns.x_send[x * x_rows + y * row_share:x * x_rows + (y + 1) * row_share] = (
+                    ns.part[core, rows] + ns.other[rows]
+                ).astype(BF16)
+            start_all("table", nx, x_rows, ns.x_send, ns.x_recv, ns.send.at[3], ns.recv.at[3], lo=lax.div(table, nx) * nx)
 
     first = (("table", n_table, n_dp * cap), ("dp", n_dp, n_table * cap))
     second = first[::-1]
@@ -349,14 +358,6 @@
     hop_one(0, 1)
     hop_one(1, 1)
 
-    to_core.wait_recv()
-    for t in range(n_table):
-        y, x = t // nx, t % nx
-        rows = slice(t * row_share, (t + 1) * row_share)
-        ns.x_send[x * x_rows + y * row_share:x * x_rows + (y + 1) * row_share] = (
-            ns.part[core, rows] + ns.other[rows]
-        ).astype(BF16)
-    start_all("table", nx, x_rows, ns.x_send, ns.x_recv, ns.send.at[3], ns.recv.at[3], lo=lax.div(table, nx) * nx)
     wait_bytes(ns.meta.at[1], ns.recv.at[0])
     ns.meta[2] = dot_nn(swap_rows(n_table, n_dp, 1), ns.meta[1]).astype(BF16)
     start_all("dp", n_dp, n_table, ns.meta.at[2], ns.meta.at[3], ns.send.at[1], ns.recv.at[1])
@@ -372,6 +373,9 @@
 
     hop_two(0, 0)
     hop_two(1, 0)
+
+    hop_two(0, 1)
+    hop_two(1, 1)
 
     wait_bytes(ns.y_recv, ns.recv.at[4])
     share = ns.y_recv[0:row_share].astype(F32)
@@ -403,9 +407,6 @@
     items = item_lanes(ns.meta[3], n_dp, n_table)
     ns.item_rows[0:1, :] = items[0]
     ns.item_rows[1:2, :] = items[1]
-
-    hop_two(0, 1)
-    hop_two(1, 1)
 
     wait_bytes(ns.fin_recv, ns.recv.at[5])
     total = ns.fin_recv[0]

time: 66.4 us -> 63.1 us (0.950)
  Pallas kernels: 65.3 us -> 62.1 us
    pallas_call x1, Pallas kernels: 60.4 us -> 57.2 us  [local(): pl.pallas_call(functools.partial(kernel, n_dp, n_table), out_shape=(block...]
where the time goes in v4:
time: 63.1 us; the launch traced here: 62.9 us
  Pallas kernels  62.1 us (98%)
  between operations  0.8 us (1%)
    pallas_call x1, Pallas kernels, local(): pl.pallas_call(functools.partial(kernel, n_dp, n_table), out_shape=(block...  57.2 us
    pallas_call x1, Pallas kernels, local(): pl.pallas_call(place_kernel, out_shape=(block, jax.ShapeDtypeStruct((ROWS...  4.91 us

profile of v4, /device:TPU:1, one launch (start us, length us, event | category | flops | bytes accessed | tf_op | source)
XLA Modules:
  0.0 62.9 jit_solution(7239610493772893931)
XLA Ops:
  0.6 57.2 %shard_map.86 = (f32[16,32]{1,0:T(8,128)}, s32[8,1024]{1,0:T(8,128)}, bf16[2,1024,256]{2,1,0:T(8,128)(2,1)}) custom-call(bf16[512,512]{1,0:T(8,128)(2,1)} %refs_0_.1, bf16[512,512]{1,0:T(8,128)(2,1)} %refs_1_.1, bf16[512,2048]{1,0:T(8,128)(2,1)} %refs_2_.1, bf16[512,512]{1,0:T(8,128)(2,1)} %refs_3_.1, s32[1,8]{1,0:T(1,128)} %refs_4_.1, s32[1,512]{1,0:T(1,128)} %bitcast.2, ...), custom_call_target="tpu_custom_call" | custom-call | tf_op jit(solution)/shard_map/pallas_call | solution.py:527
  57.8 4.9 %shard_map.87 = (f32[16,32]{1,0:T(8,128)}, bf16[1024,512]{1,0:T(8,128)(2,1)}) custom-call(bf16[2,1024,256]{2,1,0:T(8,128)(2,1)} %get-tuple-element.5.arrived_ref, s32[8,1024]{1,0:T(8,128)} %get-tuple-element.6.item_ref, f32[16,32]{1,0:T(8,128)} %get-tuple-element.7.block_ref), custom_call_target="tpu_custom_call" | custom-call | tf_op jit(solution)/shard_map/pallas_call | solution.py:541

commit v5 on v4

--- a/solution.py
+++ b/solution.py
@@ -31,17 +31,13 @@
 
 
 def build_bias(len_ref, bias_ref):
-    ends, total = [], 0
-    for n in range(8):
-        total = total + len_ref[0, n]
-        ends.append(total)
+    lengths = len_ref[...]
+    upto = lax.broadcasted_iota(jnp.int32, (8, 8), 1) <= lax.broadcasted_iota(jnp.int32, (8, 8), 0)
+    ends = jnp.sum(jnp.where(upto, lengths.astype(F32), 0.0), axis=1, keepdims=True).astype(jnp.int32)
     col = lax.broadcasted_iota(jnp.int32, (TOK, 1), 0)
     row = lax.broadcasted_iota(jnp.int32, (1, TOK), 1)
-    seg_col = jnp.zeros((TOK, 1), jnp.int32)
-    seg_row = jnp.zeros((1, TOK), jnp.int32)
-    for n in range(8):
-        seg_col = seg_col + (col >= ends[n]).astype(jnp.int32)
-        seg_row = seg_row + (row >= ends[n]).astype(jnp.int32)
+    seg_row = jnp.sum(jnp.where(row >= ends, 1.0, 0.0), axis=0, keepdims=True)
+    seg_col = jnp.broadcast_to(seg_row, (128, TOK)).T[:, 0:1]
     for jb in range(TOK // JB):
         lo, hi = window(jb)
         keep = (seg_col[lo:lo + JB] == seg_row[:, lo:hi]) & (col[lo:lo + JB] <= row[:, lo:hi])
@@ -190,16 +186,20 @@
     return jnp.where(at == cols_of, 1.0, 0.0).astype(BF16)
 
 
+def block_at(n, rows):
+    return pl.ds(pl.multiple_of(n * rows, rows), rows) if rows > 1 else pl.ds(n, 1)
+
+
 def start_all(axis, size, rows, src_ref, dst_ref, send_sem, recv_sem, lo=0, step=1):
     at = lax.axis_index(axis)
     me = lax.div(at - lo, step)
-    mine = pl.ds(pl.multiple_of(me * rows, rows), rows)
+    mine = block_at(me, rows)
     pltpu.make_async_copy(src_ref.at[mine], dst_ref.at[mine], recv_sem).start()
 
     def send(k, carry):
         peer = lax.rem(me + k, size)
         pltpu.make_async_remote_copy(
-            src_ref=src_ref.at[pl.ds(pl.multiple_of(peer * rows, rows), rows)],
+            src_ref=src_ref.at[block_at(peer, rows)],
             dst_ref=dst_ref.at[mine],
             send_sem=send_sem,
             recv_sem=recv_sem,
@@ -228,10 +228,30 @@
     oh_a[...] = one_hot(SLOTS, table * (n_dp * cap) + dp * cap + rank)
     oh_b[...] = one_hot(SLOTS, dp * (n_table * cap) + table * cap + rank)
     code = item_ref[...] + 1
-    line = lax.broadcasted_iota(jnp.int32, (128, TOK), 0)
-    words = jnp.where((line & 1) == 0, code >> 5, code & 31).astype(F32)
-    meta_t = jnp.where((line >> 1) == rank, words, 0.0).astype(BF16)
-    meta_ref[...] = dot_nt(one_hot(pairs, table * n_dp + dp), meta_t).astype(BF16)
+    to_table = one_hot(n_table, table).astype(F32)
+    lane = one_hot(meta_ref.shape[1], dp * cap + rank)
+    high, low = (dot_nt((to_table * word.astype(F32)).astype(BF16), lane) for word in (code >> 5, code & 31))
+    meta_ref[...] = high * 32.0 + low
+
+
+def words(values):
+    whole = values.astype(jnp.int32)
+    return (whole >> 5).astype(F32).astype(BF16), (whole & 31).astype(F32).astype(BF16)
+
+
+def turn_items(landed, n_dp, cap):
+    n_table, lanes = landed.shape
+    row = lax.broadcasted_iota(jnp.int32, (lanes, 1), 0)
+    col = lax.broadcasted_iota(jnp.int32, (1, lanes), 1)
+    spread = one_hot(n_table, col >> log2(cap))
+    gather = jnp.where((lax.broadcasted_iota(jnp.int32, (n_dp, lanes), 0)) == (
+        lax.broadcasted_iota(jnp.int32, (n_dp, lanes), 1) >> log2(cap)), 1.0, 0.0).astype(BF16)
+    parts = []
+    for word in words(landed):
+        turned = dot_nn(word.astype(F32).T.astype(BF16), spread)
+        kept = jnp.where((row & (cap - 1)) == (col & (cap - 1)), turned, 0.0).astype(BF16)
+        parts.append(dot_nn(gather, kept))
+    return parts[0] * 32.0 + parts[1]
 
 
 def swap_rows(first, second, cap):
@@ -244,20 +264,17 @@
     return jnp.where(at == a * (second * cap) + b * cap + slot, 1.0, 0.0).astype(BF16)
 
 
-def item_lanes(meta, n_dp, n_table):
-    pairs = n_dp * n_table
-    cap = SLOTS // pairs
-    lines = meta.astype(F32).T.astype(BF16)
+def item_lanes(turned, n_dp, n_table):
+    cap = SLOTS // (n_dp * n_table)
     col = lax.broadcasted_iota(jnp.int32, (1, SLOTS), 1)
-    word = lax.broadcasted_iota(jnp.int32, (128, SLOTS), 0)
+    row = lax.broadcasted_iota(jnp.int32, (n_dp, SLOTS), 0)
     slot, pair = col & (cap - 1), col >> log2(cap)
-    other = (pair & (n_dp - 1)) * n_table + (pair >> log2(n_dp))
+    high, low = words(turned)
     items = []
-    for order in (pair, other):
-        spread = dot_nn(lines, one_hot(pairs, order))
-        high = jnp.sum(jnp.where(word == 2 * slot, spread, 0.0), axis=0, keepdims=True)
-        low = jnp.sum(jnp.where(word == 2 * slot + 1, spread, 0.0), axis=0, keepdims=True)
-        items.append((high * 32.0 + low - 1.0).astype(jnp.int32))
+    for dp, table in ((pair >> log2(n_table), pair & (n_table - 1)), (pair & (n_dp - 1), pair >> log2(n_dp))):
+        spread = one_hot(turned.shape[1], table * cap + slot)
+        every = dot_nn(high, spread) * 32.0 + dot_nn(low, spread)
+        items.append((jnp.sum(jnp.where(row == dp, every, 0.0), axis=0, keepdims=True) - 1.0).astype(jnp.int32))
     return items
 
 
@@ -273,6 +290,13 @@
     row_share, col_share, half_dp = D // n_table, D // n_dp, n_dp // 2
     x_rows = ny * row_share
 
+    loads = {}
+    for n, name in enumerate(INPUTS):
+        held = getattr(ns, name + "_v")
+        held = held.at[pl.ds(0, D)] if name == "w_in" else held
+        loads[name] = pltpu.make_async_copy(getattr(ns, name), held, ns.load.at[n])
+        loads[name].start()
+
     barrier = pltpu.get_barrier_semaphore()
     for axis, size, me in (("table", n_table, table), ("dp", n_dp, dp)):
         def greet(k, carry, axis=axis, size=size, me=me):
@@ -282,19 +306,15 @@
             return carry
         lax.fori_loop(1, size, greet, 0)
 
-    loads = {}
-    for n, name in enumerate(("events", "w_in", "w_out", "upstream")):
-        held = getattr(ns, name + "_v")
-        held = held.at[pl.ds(0, D)] if name == "w_in" else held
-        loads[name] = pltpu.make_async_copy(getattr(ns, name), held, ns.load.at[n])
-        loads[name].start()
-
-    route_slots(ns.owners, ns.items, n_dp, n_table, ns.oh_a, ns.oh_b, ns.meta.at[0])
-    build_bias(ns.lengths, ns.bias)
     zero_corners(ns.w, (HEADS,))
     zero_corners(ns.ds, ())
+    loads["lengths"].wait()
+    build_bias(ns.lengths_v, ns.bias)
     loads["events"].wait()
     normalize_events(ns.events_v, ns.xnt, ns.normedt, ns.inv)
+    loads["owners"].wait()
+    loads["items"].wait()
+    route_slots(ns.owners_v, ns.items_v, n_dp, n_table, ns.oh_a, ns.oh_b, ns.item_send)
     loads["w_in"].wait()
     project(ns.w_in_v, ns.normedt, ns.slope, ns.act, ns.half)
     sum_rows(ns.w_in_v)
@@ -306,7 +326,7 @@
     for half in range(2):
         ns.part[half] = dot_nn(ns.gated[...], ns.upstream_v[:, half * 256:half * 256 + 256])
     pl.semaphore_wait(barrier, n_table + n_dp - 2)
-    start_all("table", n_table, n_dp, ns.meta.at[0], ns.meta.at[1], ns.send.at[0], ns.recv.at[0])
+    start_all("table", n_table, 1, ns.item_send, ns.item_land, ns.send.at[0], ns.recv.at[0])
     to_core = pltpu.make_async_remote_copy(
         src_ref=ns.part.at[1 - core],
         dst_ref=ns.other,
@@ -358,9 +378,9 @@
     hop_one(0, 1)
     hop_one(1, 1)
 
-    wait_bytes(ns.meta.at[1], ns.recv.at[0])
-    ns.meta[2] = dot_nn(swap_rows(n_table, n_dp, 1), ns.meta[1]).astype(BF16)
-    start_all("dp", n_dp, n_table, ns.meta.at[2], ns.meta.at[3], ns.send.at[1], ns.recv.at[1])
+    wait_bytes(ns.item_land, ns.recv.at[0])
+    ns.item_again[...] = turn_items(ns.item_land[...], n_dp, cap)
+    start_all("dp", n_dp, 1, ns.item_again, ns.item_done, ns.send.at[1], ns.recv.at[1])
     ns.swap_a[...] = swap_rows(n_table, n_dp, cap)
     ns.swap_b[...] = swap_rows(n_dp, n_table, cap)
 
@@ -403,8 +423,8 @@
                 device_id_type=MESH,
             ).start()
 
-    wait_bytes(ns.meta.at[3], ns.recv.at[1])
-    items = item_lanes(ns.meta[3], n_dp, n_table)
+    wait_bytes(ns.item_done, ns.recv.at[1])
+    items = item_lanes(ns.item_done[...], n_dp, n_table)
     ns.item_rows[0:1, :] = items[0]
     ns.item_rows[1:2, :] = items[1]
 
@@ -418,8 +438,8 @@
         block = jnp.where(lane == at, total[:, at:at + col_share], block)
     ns.grad_block[...] = block
 
-    wait_bytes(ns.meta.at[0, pl.ds(0, (n_table - 1) * n_dp)], ns.send.at[0])
-    wait_bytes(ns.meta.at[2, pl.ds(0, (n_dp - 1) * n_table)], ns.send.at[1])
+    wait_bytes(ns.item_send.at[pl.ds(0, n_table - 1)], ns.send.at[0])
+    wait_bytes(ns.item_again.at[pl.ds(0, n_dp - 1)], ns.send.at[1])
     to_core.wait_send()
     wait_bytes(ns.x_send.at[pl.ds(0, (nx - 1) * x_rows)], ns.send.at[3])
     if ny > 1:
@@ -439,37 +459,44 @@
             wait_bytes(ns.arrived.at[path, :, pl.ds(half * 128, 128)], ns.hop_recv.at[path, half, 1])
 
 
-def place_kernel(arrived_ref, item_ref, block_ref, out_ref, table_ref, rows, built, load, store):
-    copies = [pltpu.make_async_copy(arrived_ref.at[p], rows.at[p], load.at[p]) for p in range(2)]
+def place_kernel(arrived_ref, item_ref, block_ref, out_ref, table_ref, rows, items, built, load, store):
+    copies = [pltpu.make_async_copy(item_ref, items, load.at[2])]
+    copies += [pltpu.make_async_copy(arrived_ref.at[p], rows.at[p], load.at[p]) for p in range(2)]
+    block_copy = pltpu.make_async_copy(block_ref, out_ref, load.at[3])
     for copy in copies:
         copy.start()
-    out_ref[...] = block_ref[...]
+    block_copy.start()
+    copies[0].wait()
     blocks = built.shape[0]
     size = ROWS_DEV // blocks
     stores = []
     for b in range(blocks):
         for p in range(2):
-            hits = one_hot(size, item_ref[p:p + 1, :] - b * size)
+            hits = one_hot(size, items[p:p + 1, :] - b * size)
             if b == 0:
-                copies[p].wait()
+                copies[p + 1].wait()
             built[b, :, 256 - p * 256:512 - p * 256] = dot_nn(hits, rows[p]).astype(BF16)
         stores.append(pltpu.make_async_copy(built.at[b], table_ref.at[pl.ds(b * size, size)], store.at[b]))
         stores[-1].start()
+    block_copy.wait()
     for copy in stores:
         copy.wait()
 
 
-INPUTS = ("events", "upstream", "w_in", "w_out", "lengths", "owners", "items")
+INPUTS = ("events", "lengths", "owners", "items", "w_in", "upstream", "w_out")
 OUTPUTS = ("grad_block", "item_rows", "arrived")
 
 
 def scratch(n_dp, n_table):
     row_share = D // n_table
-    pairs = n_dp * n_table
+    item_lane = max(128, SLOTS // min(n_dp, n_table))
     vmem = pltpu.VMEM
     dma = pltpu.SemaphoreType.DMA
     return dict(
         events_v=vmem((TOK, D), BF16),
+        lengths_v=vmem((1, 8), jnp.int32),
+        owners_v=vmem((1, TOK), jnp.int32),
+        items_v=vmem((1, TOK), jnp.int32),
         upstream_v=vmem((TOK, D), BF16),
         w_in_v=vmem((D + 16, 4 * D), BF16),
         half=vmem((4 * D, TOK), F32),
@@ -495,7 +522,10 @@
         oh_b=vmem((SLOTS, TOK), BF16),
         swap_a=vmem((SLOTS, SLOTS), BF16),
         swap_b=vmem((SLOTS, SLOTS), BF16),
-        meta=vmem((4, pairs, 128), BF16),
+        item_send=vmem((n_table, item_lane), F32),
+        item_land=vmem((n_table, item_lane), F32),
+        item_again=vmem((n_dp, item_lane), F32),
+        item_done=vmem((n_dp, item_lane), F32),
         moved=vmem((2, SLOTS, 256), BF16),
         landed=vmem((2, 2, SLOTS, 128), BF16),
         again=vmem((2, 2, SLOTS, 128), BF16),
@@ -507,7 +537,7 @@
         y_recv=vmem((D // 4, 256), BF16),
         fin_send=vmem((2, row_share, 128), F32),
         fin_recv=vmem((n_dp // 2, row_share, 128), F32),
-        load=dma((4,)),
+        load=dma((len(INPUTS),)),
         send=dma((6,)),
         recv=dma((6,)),
         hop_send=dma((2, 2, 2)),
@@ -519,7 +549,6 @@
 def solution(mesh):
     n_dp, n_table = mesh.shape["dp"], mesh.shape["table"]
     in_vmem = pl.BlockSpec(memory_space=pltpu.VMEM)
-    in_smem = pl.BlockSpec(memory_space=pltpu.SMEM)
     anywhere = pl.BlockSpec(memory_space=pl.ANY)
 
     def local(events, upstream, w_in, w_out, lengths, owners, item_rows):
@@ -531,22 +560,23 @@
                 jax.ShapeDtypeStruct((8, SLOTS), jnp.int32),
                 jax.ShapeDtypeStruct((2, SLOTS, 256), BF16),
             ),
-            in_specs=[anywhere] * 4 + [in_smem] + [in_vmem] * 2,
+            in_specs=[anywhere] * len(INPUTS),
             out_specs=(in_vmem, in_vmem, anywhere),
             scratch_shapes=list(scratch(n_dp, n_table).values()),
             compiler_params=pltpu.CompilerParams(
                 collective_id=0, has_side_effects=True, vmem_limit_bytes=60 << 20
             ),
-        )(events, upstream, w_in, w_out, lengths, owners.reshape(1, TOK), item_rows.reshape(1, TOK))
+        )(events, lengths, owners.reshape(1, TOK), item_rows.reshape(1, TOK), w_in, upstream, w_out)
         return pl.pallas_call(
             place_kernel,
             out_shape=(block, jax.ShapeDtypeStruct((ROWS_DEV, D), BF16)),
-            in_specs=[anywhere, in_vmem, in_vmem],
-            out_specs=(in_vmem, anywhere),
+            in_specs=[anywhere] * 3,
+            out_specs=(anywhere, anywhere),
             scratch_shapes=[
                 pltpu.VMEM((2, SLOTS, 256), BF16),
+                pltpu.VMEM((8, SLOTS), jnp.int32),
                 pltpu.VMEM((PLACE_BLOCKS, ROWS_DEV // PLACE_BLOCKS, D), BF16),
-                pltpu.SemaphoreType.DMA((2,)),
+                pltpu.SemaphoreType.DMA((4,)),
                 pltpu.SemaphoreType.DMA((PLACE_BLOCKS,)),
             ],
             compiler_params=pltpu.CompilerParams(vmem_limit_bytes=60 << 20),

time: 63.1 us -> 60.8 us (0.964)
  Pallas kernels: 62.1 us -> 59.8 us
    pallas_call x1, Pallas kernels: 4.91 us -> 3.59 us  [local(): pl.pallas_call(place_kernel, out_shape=(block, jax.ShapeDtypeStruct((ROWS...]
    pallas_call x1, Pallas kernels: 57.2 us -> 56.2 us  [local(): pl.pallas_call(functools.partial(kernel, n_dp, n_table), out_shape=(block...]
where the time goes in v5:
time: 60.8 us; the launch traced here: 60.6 us
  Pallas kernels  59.8 us (98%)
  between operations  0.8 us (1%)
    pallas_call x1, Pallas kernels, local(): pl.pallas_call(functools.partial(kernel, n_dp, n_table), out_shape=(block...  56.2 us
    pallas_call x1, Pallas kernels, local(): pl.pallas_call(place_kernel, out_shape=(block, jax.ShapeDtypeStruct((ROWS...  3.59 us

profile of v5, /device:TPU:1, one launch (start us, length us, event | category | flops | bytes accessed | tf_op | source)
XLA Modules:
  0.0 60.6 jit_solution(13184543244680735482)
XLA Ops:
  0.6 56.2 %shard_map.86 = (f32[16,32]{1,0:T(8,128)}, s32[8,1024]{1,0:T(8,128)}, bf16[2,1024,256]{2,1,0:T(8,128)(2,1)}) custom-call(bf16[512,512]{1,0:T(8,128)(2,1)} %refs_0_.1, s32[1,8]{1,0:T(1,128)} %refs_1_.1, s32[1,512]{1,0:T(1,128)} %bitcast.2, s32[1,512]{1,0:T(1,128)} %bitcast.3, bf16[512,2048]{1,0:T(8,128)(2,1)} %refs_4_.1, bf16[512,512]{1,0:T(8,128)(2,1)} %refs_5_.1, ...), custom_call_target="tpu_custom_call" | custom-call | tf_op jit(solution)/shard_map/pallas_call | solution.py:556
  56.9 3.6 %shard_map.87 = (f32[16,32]{1,0:T(8,128)}, bf16[1024,512]{1,0:T(8,128)(2,1)}) custom-call(bf16[2,1024,256]{2,1,0:T(8,128)(2,1)} %get-tuple-element.5.arrived_ref, s32[8,1024]{1,0:T(8,128)} %get-tuple-element.6.item_ref, f32[16,32]{1,0:T(8,128)} %get-tuple-element.7.block_ref), custom_call_target="tpu_custom_call" | custom-call | tf_op jit(solution)/shard_map/pallas_call | solution.py:570

commit v6 on v5

--- a/solution.py
+++ b/solution.py
@@ -13,7 +13,7 @@
 EPS = 1e-6
 F32 = jnp.float32
 BF16 = jnp.bfloat16
-JB = 128
+JB = 256
 OUT_OF_MASK = -1e30
 
 
@@ -42,14 +42,6 @@
         lo, hi = window(jb)
         keep = (seg_col[lo:lo + JB] == seg_row[:, lo:hi]) & (col[lo:lo + JB] <= row[:, lo:hi])
         bias_ref[lo:lo + JB, lo:hi] = jnp.where(keep, 0.0, OUT_OF_MASK)
-
-
-def zero_corners(ref, lead):
-    zeros = jnp.zeros(lead + (128, 128), ref.dtype)
-    full = (slice(None),) * len(lead)
-    ref[full + (slice(0, 128), slice(384, 512))] = zeros
-    ref[full + (slice(128, 256), slice(0, 128))] = zeros
-    ref[full + (slice(384, 512), slice(256, 384))] = zeros
 
 
 def normalize_events(ev_ref, xnt_ref, normedt_ref, inv_ref):
@@ -157,13 +149,13 @@
     w_in_ref[D:D + 16, :] = jnp.concatenate([high, (sums - high.astype(F32)).astype(BF16)], axis=0)
 
 
-def event_gradient(path, w_in_ref, zg_ref, dot_ref, stat_ref, upt_ref, xnt_ref, inv_ref):
-    if path == 0:
+def event_gradient(part, w_in_ref, zg_ref, dot_ref, stat_ref, upt_ref, xnt_ref, inv_ref):
+    if part == 1:
+        at = slice(256, 512)
         ng = dot_nn(w_in_ref[256:D + 16, :], zg_ref[...])
         stat_ref[0:1, :] = (ng[256:257] + ng[264:265]) * (1.0 / 512.0)
         stat_ref[1:2, :] = dot_ref[...] * (1.0 / 256.0)
         ng = ng[0:256]
-        at = slice(256, 512)
     else:
         at = slice(0, 256)
         ng = dot_nn(w_in_ref[at, :], zg_ref[...])
@@ -306,8 +298,6 @@
             return carry
         lax.fori_loop(1, size, greet, 0)
 
-    zero_corners(ns.w, (HEADS,))
-    zero_corners(ns.ds, ())
     loads["lengths"].wait()
     build_bias(ns.lengths_v, ns.bias)
     loads["events"].wait()
@@ -371,12 +361,12 @@
             ns.hop_send.at[path, half, 1], ns.hop_recv.at[path, half, 1],
         )
 
-    for path, slots in ((0, ns.oh_a), (1, ns.oh_b)):
-        grad = event_gradient(path, ns.w_in_v, ns.zg, ns.dot, ns.stat, ns.upt, ns.xnt, ns.inv)
-        ns.moved[path] = dot_nt(slots[...], grad).astype(BF16)
-        hop_one(path, 0)
-    hop_one(0, 1)
-    hop_one(1, 1)
+    for part in (1, 0):
+        grad = event_gradient(part, ns.w_in_v, ns.zg, ns.dot, ns.stat, ns.upt, ns.xnt, ns.inv)
+        for path, slots in ((0, ns.oh_a), (1, ns.oh_b)):
+            lo = 128 if path != part else 0
+            ns.moved[path, :, part * 128:part * 128 + 128] = dot_nt(slots[...], grad[lo:lo + 128]).astype(BF16)
+            hop_one(path, part)
 
     wait_bytes(ns.item_land, ns.recv.at[0])
     ns.item_again[...] = turn_items(ns.item_land[...], n_dp, cap)
@@ -391,32 +381,35 @@
     ns.y_send[...] = share.astype(BF16)
     start_all("table", ny, row_share, ns.y_send, ns.y_recv, ns.send.at[4], ns.recv.at[4], lo=lax.rem(table, nx), step=nx)
 
+    hop_two(0, 1)
+    hop_two(1, 1)
+
     hop_two(0, 0)
     hop_two(1, 0)
-
-    hop_two(0, 1)
-    hop_two(1, 1)
 
     wait_bytes(ns.y_recv, ns.recv.at[4])
     share = ns.y_recv[0:row_share].astype(F32)
     for y in range(1, ny):
         share = share + ns.y_recv[y * row_share:(y + 1) * row_share].astype(F32)
-    for g in range(2):
-        ns.fin_send[g] = share[:, g * 128:g * 128 + 128]
+    for m in range(half_dp):
+        cols = share[:, m * col_share:(m + 1) * col_share]
+        if col_share < 128:
+            cols = jnp.concatenate([cols, jnp.zeros((row_share, 128 - col_share), F32)], axis=1)
+        ns.fin_send[m] = cols
     z = lax.div(dp, 2)
     for m in range(half_dp):
         target = core * half_dp + m
-        group = ns.fin_send.at[m * col_share // 128]
+        group = ns.fin_send.at[m]
 
         @pl.when(target == dp)
         def _():
-            pltpu.make_async_copy(group, ns.fin_recv.at[z], ns.recv.at[5]).start()
+            pltpu.make_async_copy(group, ns.grad_parts.at[z], ns.recv.at[5]).start()
 
         @pl.when(target != dp)
         def _():
             pltpu.make_async_remote_copy(
                 src_ref=group,
-                dst_ref=ns.fin_recv.at[z],
+                dst_ref=ns.grad_parts.at[z],
                 send_sem=ns.fin_sem.at[m],
                 recv_sem=ns.recv.at[5],
                 device_id={"dp": target},
@@ -425,19 +418,12 @@
 
     wait_bytes(ns.item_done, ns.recv.at[1])
     items = item_lanes(ns.item_done[...], n_dp, n_table)
-    ns.item_rows[0:1, :] = items[0]
-    ns.item_rows[1:2, :] = items[1]
-
-    wait_bytes(ns.fin_recv, ns.recv.at[5])
-    total = ns.fin_recv[0]
-    for k in range(1, half_dp):
-        total = total + ns.fin_recv[k]
-    lane = lax.rem(lax.rem(dp, half_dp) * col_share, 128)
-    block = total[:, 0:col_share]
-    for at in range(col_share, 128, col_share):
-        block = jnp.where(lane == at, total[:, at:at + col_share], block)
-    ns.grad_block[...] = block
-
+    ns.item_rows_v[0:1, :] = items[0]
+    ns.item_rows_v[1:2, :] = items[1]
+    keep_items = pltpu.make_async_copy(ns.item_rows_v, ns.item_rows, ns.keep)
+    keep_items.start()
+
+    keep_items.wait()
     wait_bytes(ns.item_send.at[pl.ds(0, n_table - 1)], ns.send.at[0])
     wait_bytes(ns.item_again.at[pl.ds(0, n_dp - 1)], ns.send.at[1])
     to_core.wait_send()
@@ -449,7 +435,7 @@
 
         @pl.when(target != dp)
         def _():
-            wait_bytes(ns.fin_send.at[m * col_share // 128], ns.fin_sem.at[m])
+            wait_bytes(ns.fin_send.at[m], ns.fin_sem.at[m])
     for half in range(2):
         for path in range(2):
             for hop, (_, size, rows) in enumerate((first[path], second[path])):
@@ -457,15 +443,15 @@
     for half in range(2):
         for path in range(2):
             wait_bytes(ns.arrived.at[path, :, pl.ds(half * 128, 128)], ns.hop_recv.at[path, half, 1])
-
-
-def place_kernel(arrived_ref, item_ref, block_ref, out_ref, table_ref, rows, items, built, load, store):
+    wait_bytes(ns.grad_parts, ns.recv.at[5])
+
+
+def place_kernel(parts_ref, item_ref, arrived_ref, out_ref, table_ref, parts, items, rows, block, built, load, store):
     copies = [pltpu.make_async_copy(item_ref, items, load.at[2])]
     copies += [pltpu.make_async_copy(arrived_ref.at[p], rows.at[p], load.at[p]) for p in range(2)]
-    block_copy = pltpu.make_async_copy(block_ref, out_ref, load.at[3])
+    copies += [pltpu.make_async_copy(parts_ref, parts, load.at[3])]
     for copy in copies:
         copy.start()
-    block_copy.start()
     copies[0].wait()
     blocks = built.shape[0]
     size = ROWS_DEV // blocks
@@ -475,16 +461,26 @@
             hits = one_hot(size, items[p:p + 1, :] - b * size)
             if b == 0:
                 copies[p + 1].wait()
-            built[b, :, 256 - p * 256:512 - p * 256] = dot_nn(hits, rows[p]).astype(BF16)
+            placed = dot_nn(hits, rows[p]).astype(BF16)
+            low, high = (0, 384) if p == 0 else (128, 256)
+            built[b, :, low:low + 128] = placed[:, 0:128]
+            built[b, :, high:high + 128] = placed[:, 128:256]
         stores.append(pltpu.make_async_copy(built.at[b], table_ref.at[pl.ds(b * size, size)], store.at[b]))
         stores[-1].start()
-    block_copy.wait()
+        if b == 0:
+            copies[3].wait()
+            total = parts[0]
+            for k in range(1, parts.shape[0]):
+                total = total + parts[k]
+            block[...] = total[:, 0:block.shape[1]]
+            stores.append(pltpu.make_async_copy(block, out_ref, store.at[blocks]))
+            stores[-1].start()
     for copy in stores:
         copy.wait()
 
 
 INPUTS = ("events", "lengths", "owners", "items", "w_in", "upstream", "w_out")
-OUTPUTS = ("grad_block", "item_rows", "arrived")
+OUTPUTS = ("grad_parts", "item_rows", "arrived")
 
 
 def scratch(n_dp, n_table):
@@ -535,9 +531,10 @@
         x_recv=vmem((D, 256), BF16),
         y_send=vmem((D // 4, 256), BF16),
         y_recv=vmem((D // 4, 256), BF16),
-        fin_send=vmem((2, row_share, 128), F32),
-        fin_recv=vmem((n_dp // 2, row_share, 128), F32),
+        fin_send=vmem((n_dp // 2, row_share, 128), F32),
+        item_rows_v=vmem((8, SLOTS), jnp.int32),
         load=dma((len(INPUTS),)),
+        keep=dma(()),
         send=dma((6,)),
         recv=dma((6,)),
         hop_send=dma((2, 2, 2)),
@@ -548,20 +545,19 @@
 
 def solution(mesh):
     n_dp, n_table = mesh.shape["dp"], mesh.shape["table"]
-    in_vmem = pl.BlockSpec(memory_space=pltpu.VMEM)
     anywhere = pl.BlockSpec(memory_space=pl.ANY)
 
     def local(events, upstream, w_in, w_out, lengths, owners, item_rows):
-        block = jax.ShapeDtypeStruct((D // n_table, D // n_dp), F32)
-        grad_block, items, arrived = pl.pallas_call(
+        row_share, col_share = D // n_table, D // n_dp
+        exchanged = pl.pallas_call(
             functools.partial(kernel, n_dp, n_table),
             out_shape=(
-                block,
+                jax.ShapeDtypeStruct((n_dp // 2, row_share, 128), F32),
                 jax.ShapeDtypeStruct((8, SLOTS), jnp.int32),
                 jax.ShapeDtypeStruct((2, SLOTS, 256), BF16),
             ),
             in_specs=[anywhere] * len(INPUTS),
-            out_specs=(in_vmem, in_vmem, anywhere),
+            out_specs=[anywhere] * 3,
             scratch_shapes=list(scratch(n_dp, n_table).values()),
             compiler_params=pltpu.CompilerParams(
                 collective_id=0, has_side_effects=True, vmem_limit_bytes=60 << 20
@@ -569,18 +565,23 @@
         )(events, lengths, owners.reshape(1, TOK), item_rows.reshape(1, TOK), w_in, upstream, w_out)
         return pl.pallas_call(
             place_kernel,
-            out_shape=(block, jax.ShapeDtypeStruct((ROWS_DEV, D), BF16)),
+            out_shape=(
+                jax.ShapeDtypeStruct((row_share, col_share), F32),
+                jax.ShapeDtypeStruct((ROWS_DEV, D), BF16),
+            ),
             in_specs=[anywhere] * 3,
             out_specs=(anywhere, anywhere),
             scratch_shapes=[
+                pltpu.VMEM((n_dp // 2, row_share, 128), F32),
+                pltpu.VMEM((8, SLOTS), jnp.int32),
                 pltpu.VMEM((2, SLOTS, 256), BF16),
-                pltpu.VMEM((8, SLOTS), jnp.int32),
+                pltpu.VMEM((row_share, col_share), F32),
                 pltpu.VMEM((PLACE_BLOCKS, ROWS_DEV // PLACE_BLOCKS, D), BF16),
                 pltpu.SemaphoreType.DMA((4,)),
-                pltpu.SemaphoreType.DMA((PLACE_BLOCKS,)),
+                pltpu.SemaphoreType.DMA((PLACE_BLOCKS + 1,)),
             ],
             compiler_params=pltpu.CompilerParams(vmem_limit_bytes=60 << 20),
-        )(arrived, items, grad_block)
+        )(*exchanged)
 
     both = P(("dp", "table"), None)
     return jax.shard_map(

time: 60.8 us -> 58.9 us (0.969)
  Pallas kernels: 59.8 us -> 58 us
    pallas_call x2, Pallas kernels: 59.8 us -> 58 us  [the longest x1 54.2 us: local(): pl.pallas_call(functools.partial(kernel, n_dp, n_table), out_shape=(jax.S...]
where the time goes in v6:
time: 58.9 us; the launch traced here: 58.8 us
  Pallas kernels  58 us (98%)
  between operations  0.8 us (1%)
    pallas_call x1, Pallas kernels, local(): pl.pallas_call(functools.partial(kernel, n_dp, n_table), out_shape=(jax.S...  54.2 us
    pallas_call x1, Pallas kernels, local(): pl.pallas_call(place_kernel, out_shape=(jax.ShapeDtypeStruct((row_share,...  3.76 us

profile of v6, /device:TPU:1, one launch (start us, length us, event | category | flops | bytes accessed | tf_op | source)
XLA Modules:
  0.0 58.8 jit_solution(6120924479980589340)
XLA Ops:
  0.6 54.2 %shard_map.86 = (f32[8,16,128]{2,1,0:T(8,128)}, s32[8,1024]{1,0:T(8,128)}, bf16[2,1024,256]{2,1,0:T(8,128)(2,1)}) custom-call(bf16[512,512]{1,0:T(8,128)(2,1)} %refs_0_.1, s32[1,8]{1,0:T(1,128)} %refs_1_.1, s32[1,512]{1,0:T(1,128)} %bitcast.2, s32[1,512]{1,0:T(1,128)} %bitcast.3, bf16[512,2048]{1,0:T(8,128)(2,1)} %refs_4_.1, bf16[512,512]{1,0:T(8,128)(2,1)} %refs_5_.1, ...), custom_call_target="tpu_custom_call" | custom-call | tf_op jit(solution)/shard_map/pallas_call | solution.py:552
  54.9 3.8 %shard_map.87 = (f32[16,32]{1,0:T(8,128)}, bf16[1024,512]{1,0:T(8,128)(2,1)}) custom-call(f32[8,16,128]{2,1,0:T(8,128)} %get-tuple-element.5.parts_ref, s32[8,1024]{1,0:T(8,128)} %get-tuple-element.6.item_ref, bf16[2,1024,256]{2,1,0:T(8,128)(2,1)} %get-tuple-element.7.arrived_ref), custom_call_target="tpu_custom_call" | custom-call | tf_op jit(solution)/shard_map/pallas_call | solution.py:566

commit v7 on v6

--- a/solution.py
+++ b/solution.py
@@ -166,7 +166,7 @@
 MESH = pl.DeviceIdType.MESH
 SLOTS = 1024
 ROWS_DEV = 1024
-PLACE_BLOCKS = 4
+PLACE_BLOCKS = 8
 
 
 def log2(n):
@@ -332,15 +332,14 @@
     att_backward(ns.w_out_v, ns.upstream_v, ns.upt, ns.att, ns.ainv, ns.act, ns.ag, z_refs)
     for h in range(HEADS):
         backward_head(h, ns.act, ns.ag, ns.w, ns.dsl, ns.ds, z_refs)
-        if h == 5:
-            to_core.wait_recv()
-            for t in range(n_table):
-                y, x = t // nx, t % nx
-                rows = slice(t * row_share, (t + 1) * row_share)
-                ns.x_send[x * x_rows + y * row_share:x * x_rows + (y + 1) * row_share] = (
-                    ns.part[core, rows] + ns.other[rows]
-                ).astype(BF16)
-            start_all("table", nx, x_rows, ns.x_send, ns.x_recv, ns.send.at[3], ns.recv.at[3], lo=lax.div(table, nx) * nx)
+    to_core.wait_recv()
+    for t in range(n_table):
+        y, x = t // nx, t % nx
+        rows = slice(t * row_share, (t + 1) * row_share)
+        ns.x_send[x * x_rows + y * row_share:x * x_rows + (y + 1) * row_share] = (
+            ns.part[core, rows] + ns.other[rows]
+        ).astype(BF16)
+    start_all("table", nx, x_rows, ns.x_send, ns.x_recv, ns.send.at[3], ns.recv.at[3], lo=lax.div(table, nx) * nx)
 
     first = (("table", n_table, n_dp * cap), ("dp", n_dp, n_table * cap))
     second = first[::-1]

time: 58.9 us -> 58.4 us (level)
  no operation moved by 1% of the time
where the time goes in v7:
time: 58.4 us; the launch traced here: 58.3 us
  Pallas kernels  57.5 us (98%)
  between operations  0.8 us (1%)
    pallas_call x1, Pallas kernels, local(): pl.pallas_call(functools.partial(kernel, n_dp, n_table), out_shape=(jax.S...  53.9 us
    pallas_call x1, Pallas kernels, local(): pl.pallas_call(place_kernel, out_shape=(jax.ShapeDtypeStruct((row_share,...  3.58 us

profile of v7, /device:TPU:1, one launch (start us, length us, event | category | flops | bytes accessed | tf_op | source)
XLA Modules:
  0.0 58.3 jit_solution(17099625941335160580)
XLA Ops:
  0.6 53.9 %shard_map.86 = (f32[8,16,128]{2,1,0:T(8,128)}, s32[8,1024]{1,0:T(8,128)}, bf16[2,1024,256]{2,1,0:T(8,128)(2,1)}) custom-call(bf16[512,512]{1,0:T(8,128)(2,1)} %refs_0_.1, s32[1,8]{1,0:T(1,128)} %refs_1_.1, s32[1,512]{1,0:T(1,128)} %bitcast.2, s32[1,512]{1,0:T(1,128)} %bitcast.3, bf16[512,2048]{1,0:T(8,128)(2,1)} %refs_4_.1, bf16[512,512]{1,0:T(8,128)(2,1)} %refs_5_.1, ...), custom_call_target="tpu_custom_call" | custom-call | tf_op jit(solution)/shard_map/pallas_call | solution.py:551
  54.5 3.6 %shard_map.87 = (f32[16,32]{1,0:T(8,128)}, bf16[1024,512]{1,0:T(8,128)(2,1)}) custom-call(f32[8,16,128]{2,1,0:T(8,128)} %get-tuple-element.5.parts_ref, s32[8,1024]{1,0:T(8,128)} %get-tuple-element.6.item_ref, bf16[2,1024,256]{2,1,0:T(8,128)(2,1)} %get-tuple-element.7.arrived_ref), custom_call_target="tpu_custom_call" | custom-call | tf_op jit(solution)/shard_map/pallas_call | solution.py:565
